TPU v7x, 32 devices: a whole 2x2x4 slice. The times are simulated.
32 devices in a mesh: ep: 16 (over z, x, core), dp: 2 (over y).
Axes of the slice: x: 2, y: 2, z: 4, core: 2. Of those that a mesh axis runs over, the one named last changes fastest.
Arguments:
- hidden: bfloat16 [4, 16, 256, 768], P('dp', 'ep'), parts along dimension 0, may hold values from -6 to 6
- down_weight: bfloat16 [16, 768, 2048], P('ep'), may hold values from -0.21875 to 0.21875
- routes: int32 [4, 256, 8], P('dp', 'ep'), parts along dimension 0, may hold values from 0 to 15, all different within a row; in each aligned block of 16 rows (0 to 15, 16 to 31, ..., all dimensions but the last counted through in order) at most 16 rows name the same one
- route_weight: float32 [4, 256, 8], P('dp', 'ep'), parts along dimension 0, may hold values from 0.03 to 0.4
- residual: bfloat16 [4, 256, 2048], P('dp', 'ep'), parts along dimension 0, may hold values from -6 to 6
Outputs:
- mixed: bfloat16 [4, 256, 2048], P('dp', 'ep'), parts along dimension 0
There are 2 independent parts, one for each index of `dp`. A program takes and returns all parts, laid end to end along the dimension named above; an argument that names none is the same for every part. Nothing has to cross between parts.
Inputs may be any that keep to these rules, and one draw needn't show every extreme that they name: `routes`: each row names 8 different experts. In each micro-batch the 16 rows of one device name no expert more than 16 times, and in every draw some device's rows name some expert exactly 16 times.
All inputs are finite; a program needn't handle non-finite values.
Results may differ from a plain program's by a relative error of at most 0.0031.
Values may be sent and summed in bfloat16 or wider, within the bound.
A program may use at most 64 MiB of HBM per device.

v0:
```python
import math

import jax
import jax.numpy as jnp
from jax import lax
from jax.sharding import PartitionSpec as P


def shards(hidden, down_weight, routes, route_weight, residual):
    ranks_total = lax.axis_size("ep")
    batch_count = routes.shape[0]
    row_count = routes.shape[1]
    choose_count = routes.shape[2]
    slot_count = hidden.shape[2]
    per_peer = slot_count // ranks_total
    model_width = down_weight.shape[2]
    matrix = down_weight[0]
    labels = jnp.arange(ranks_total, dtype=jnp.int32)
    picked = jnp.sum((routes[:, :, :, None] == labels).astype(jnp.int32), axis=2, dtype=jnp.int32)
    rank_in_block = jnp.take_along_axis(
        jnp.cumsum(picked, axis=1, dtype=jnp.int32) - picked, routes, axis=2
    )
    loads_out = jnp.transpose(jnp.sum(picked, axis=1, dtype=jnp.int32))
    loads_in = lax.all_to_all(loads_out, "ep", split_axis=0, concat_axis=0, tiled=True)
    arriving = jnp.transpose(loads_in)
    offsets = jnp.cumsum(arriving, axis=1, dtype=jnp.int32) - arriving
    totals = jnp.sum(arriving, axis=1, dtype=jnp.int32)
    results = []
    for batch_index in range(batch_count):
        packed = hidden[batch_index, 0]
        block_size = math.gcd(slot_count, 128)

        def add_block(block_index, produced_in):
            begin_at = block_index * block_size
            segment = lax.dynamic_slice_in_dim(packed, begin_at, block_size, 0)
            product = jnp.dot(segment, matrix, preferred_element_type=jnp.float32).astype(
                jnp.bfloat16
            )
            return lax.dynamic_update_slice_in_dim(produced_in, product, begin_at, 0)

        block_count = (totals[batch_index] + block_size - 1) // block_size
        expert_produced = lax.fori_loop(
            0, block_count, add_block, jnp.zeros((slot_count, model_width), jnp.bfloat16)
        )
        selector = offsets[batch_index][:, None] + jnp.arange(per_peer, dtype=jnp.int32)[None, :]
        selector = jnp.minimum(selector, slot_count - 1)
        sending = jnp.take(expert_produced, selector.reshape(-1), axis=0).reshape(
            ranks_total, per_peer, model_width
        )
        arrived = lax.all_to_all(sending, "ep", split_axis=0, concat_axis=0, tiled=True)
        flattened = arrived.reshape(ranks_total * per_peer, model_width)
        location = routes[batch_index] * per_peer + rank_in_block[batch_index]
        gathered = jnp.take(flattened, location.reshape(-1), axis=0).reshape(
            row_count, choose_count, model_width
        )
        weighted = jnp.sum(
            route_weight[batch_index][:, :, None] * gathered.astype(jnp.float32), axis=1
        )
        results.append((residual[batch_index].astype(jnp.float32) + weighted).astype(jnp.bfloat16))
    return jnp.stack(results, axis=0)


def solution(mesh):
    in_specs = (
        P("dp", "ep", None, None),
        P("ep", None, None),
        P("dp", "ep", None),
        P("dp", "ep", None),
        P("dp", "ep", None),
    )
    out_specs = P("dp", "ep", None)
    return jax.shard_map(shards, mesh=mesh, in_specs=in_specs, out_specs=out_specs, check_vma=False)
```

profile of v0, /device:TPU:0, one launch (start us, length us, event | category | flops | bytes accessed | tf_op | source)
XLA Modules:
  0.0 89.9 jit_solution(11659420845133318276)
XLA Ops:
  1.6 7.4 %all-to-all-start = ((s32[16,1,2]{2,1,0:T(1,128)}), s32[16,1,2]{2,1,0:T(1,128)S(1)}, u32[]{:S(2)}, u32[]{:S(2)}) async-start(s32[16,1,2]{2,1,0:T(1,128)} %copy.35), calls=%async_computation | async-start | bytes 16384 | tf_op jit(solution)/shard_map/all_to_all | solution.py:24
  8.9 1.2 %slice_bitcast_fusion.1 = (bf16[256,768]{1,0:T(8,128)(2,1)S(1)}, bf16[256,768]{1,0:T(8,128)(2,1)S(1)}) fusion(bf16[2,1,256,768]{3,2,1,0:T(8,128)(2,1)} %param.13), kind=kLoop, calls=%fused_computation.20 | loop fusion | bytes 1572864 | tf_op jit(solution)/shard_map/squeeze | solution.py:30
  10.2 5.2 %all-to-all-done = s32[16,1,2]{2,1,0:T(1,128)S(1)} async-done(((s32[16,1,2]{2,1,0:T(1,128)}), s32[16,1,2]{2,1,0:T(1,128)S(1)}, u32[]{:S(2)}, u32[]{:S(2)}) %all-to-all-start) | async-done | bytes 160 | tf_op jit(solution)/shard_map/all_to_all | solution.py:24
  19.1 5.0 %while.21 = (s32[]{:T(128)}, bf16[256,2048]{1,0:T(8,128)(2,1)S(1)}, s32[]{:T(128)}, bf16[256,768]{1,0:T(8,128)(2,1)S(1)}, bf16[768,2048]{1,0:T(8,128)(2,1)}, /*index=5*/s32[]{:T(128)}, s32[]{:T(128)}, s32[]{:T(128)}, s32[]{:T(128)}) while((s32[]{:T(128)}, bf16[256,2048]{1,0:T(8,128)(2,1)S(1)}, s32[]{:T(128)}, ...), condition=%wide.region_9.12_spmd, body=%wide.region_8.11_spmd.sunk | while | flops 402915328 | bytes 3867787 | solution.py:42
  19.1 2.5 %fusion.24 = bf16[256,2048]{1,0:T(8,128)(2,1)S(1)} fusion(bf16[256,2048]{1,0:T(8,128)(2,1)S(1)} %get-tuple-element.203, s32[]{:T(128)S(6)} %select_n.79, bf16[768,2048]{1,0:T(8,128)(2,1)} %get-tuple-element.215, bf16[256,768]{1,0:T(8,128)(2,1)S(1)} %get-tuple-element.214), kind=kOutput, calls=%fused_computation.10.clone.1 | convolution fusion | flops 402915328 | bytes 3867648 | tf_op jit(solution)/shard_map/while/body/dot_general | solution.py:36
  21.7 2.5 %fusion.24 = bf16[256,2048]{1,0:T(8,128)(2,1)S(1)} fusion(bf16[256,2048]{1,0:T(8,128)(2,1)S(1)} %get-tuple-element.203, s32[]{:T(128)S(6)} %select_n.79, bf16[768,2048]{1,0:T(8,128)(2,1)} %get-tuple-element.215, bf16[256,768]{1,0:T(8,128)(2,1)S(1)} %get-tuple-element.214), kind=kOutput, calls=%fused_computation.10.clone.1 | convolution fusion | flops 402915328 | bytes 3867648 | tf_op jit(solution)/shard_map/while/body/dot_general | solution.py:36
  24.2 2.4 %gather_fusion.3 = bf16[256,2048]{1,0:T(8,128)(2,1)} fusion(bf16[256,2048]{1,0:T(8,128)(2,1)S(1)} %get-tuple-element.64, s32[1024]{0:T(1024)S(1)} %pad_clamp_fusion.1), kind=kCustom, calls=%fused_computation.2.clone | custom fusion | bytes 2098176 | tf_op jit(solution)/shard_map/jit(_take)/gather | solution.py:47
  26.5 2.5 %broadcast_select_fusion = bf16[256,2048]{1,0:T(8,128)(2,1)} fusion(bf16[256,2048]{1,0:T(8,128)(2,1)} %gather_fusion.3, pred[256]{0:T(512)(128)(4,1)} %compare_and_fusion.1), kind=kLoop, calls=%fused_computation.17 | loop fusion | flops 524288 | bytes 2097408 | tf_op jit(solution)/shard_map/jit(_take)/select_n | solution.py:47
  29.1 4.3 %all-to-all-start.2 = ((bf16[16,16,2048]{2,1,0:T(8,128)(2,1)}), bf16[16,16,2048]{2,1,0:T(8,128)(2,1)}, u32[]{:S(2)}, u32[]{:S(2)}) async-start(bf16[16,16,2048]{2,1,0:T(8,128)(2,1)} %bitcast.54), calls=%async_computation.2 | async-start | bytes 2097152 | tf_op jit(solution)/shard_map/all_to_all | solution.py:50
  33.4 1.4 %min.15 = s32[256]{0:T(256)} reshape(s32[16,16]{1,0:T(8,128)} %get-tuple-element.100) | data formatting | bytes 2048 | tf_op jit(solution)/shard_map/min | solution.py:46
  36.0 1.1 %broadcast.34.clone = bf16[256,2048]{1,0:T(8,128)(2,1)} broadcast(bf16[]{:T(256)} %constant.85.clone.1), dimensions={} | broadcast | bytes 1048578 | tf_op jit(solution)/shard_map/broadcast.5
  37.2 2.8 %while.20 = (s32[]{:T(128)}, bf16[256,2048]{1,0:T(8,128)(2,1)}, s32[]{:T(128)}, bf16[256,768]{1,0:T(8,128)(2,1)S(1)}, bf16[768,2048]{1,0:T(8,128)(2,1)S(1)}, /*index=5*/s32[]{:T(128)}, s32[]{:T(128)}, s32[]{:T(128)}, s32[]{:T(128)}) while((s32[]{:T(128)}, bf16[256,2048]{1,0:T(8,128)(2,1)}, s32[]{:T(128)}, bf16[256,768]{1,0:T(8,128)(2,1)S(1)}, ...), condition=%wide.region_3.4_spmd, body=%wide.region_2.3_spmd.sunk | while | flops 402915328 | bytes 3867787 | solution.py:42
  37.2 1.4 %fusion.21 = bf16[256,2048]{1,0:T(8,128)(2,1)} fusion(bf16[256,2048]{1,0:T(8,128)(2,1)} %get-tuple-element.176, s32[]{:T(128)S(6)} %select_n.78, bf16[768,2048]{1,0:T(8,128)(2,1)S(1)} %get-tuple-element.188, bf16[256,768]{1,0:T(8,128)(2,1)S(1)} %get-tuple-element.187), kind=kOutput, calls=%fused_computation.6.clone.1 | convolution fusion | flops 402915328 | bytes 3867648 | tf_op jit(solution)/shard_map/while/body/dot_general | solution.py:36
  38.6 1.4 %fusion.21 = bf16[256,2048]{1,0:T(8,128)(2,1)} fusion(bf16[256,2048]{1,0:T(8,128)(2,1)} %get-tuple-element.176, s32[]{:T(128)S(6)} %select_n.78, bf16[768,2048]{1,0:T(8,128)(2,1)S(1)} %get-tuple-element.188, bf16[256,768]{1,0:T(8,128)(2,1)S(1)} %get-tuple-element.187), kind=kOutput, calls=%fused_computation.6.clone.1 | convolution fusion | flops 402915328 | bytes 3867648 | tf_op jit(solution)/shard_map/while/body/dot_general | solution.py:36
  39.9 3.9 %gather_fusion.1 = bf16[256,2048]{1,0:T(8,128)(2,1)S(1)} fusion(bf16[256,2048]{1,0:T(8,128)(2,1)} %get-tuple-element.63, s32[1024]{0:T(1024)} %pad_clamp_fusion.3), kind=kCustom, calls=%fused_computation.clone | custom fusion | bytes 2098176 | tf_op jit(solution)/shard_map/jit(_take)/gather | solution.py:47
  43.8 1.2 %broadcast_select_fusion.1 = bf16[256,2048]{1,0:T(8,128)(2,1)} fusion(bf16[256,2048]{1,0:T(8,128)(2,1)S(1)} %gather_fusion.1, pred[256]{0:T(512)(128)(4,1)S(1)} %compare_and_fusion.3), kind=kLoop, calls=%fused_computation.18 | loop fusion | flops 524288 | bytes 2097408 | tf_op jit(solution)/shard_map/jit(_take)/select_n | solution.py:47
  45.0 11.3 %all-to-all-done.2 = bf16[16,16,2048]{2,1,0:T(8,128)(2,1)} async-done(((bf16[16,16,2048]{2,1,0:T(8,128)(2,1)}), bf16[16,16,2048]{2,1,0:T(8,128)(2,1)}, u32[]{:S(2)}, u32[]{:S(2)}) %all-to-all-start.2) | async-done | bytes 1048608 | tf_op jit(solution)/shard_map/all_to_all | solution.py:50
  56.3 6.8 %all-to-all-start.1 = ((bf16[16,16,2048]{2,1,0:T(8,128)(2,1)}), bf16[16,16,2048]{2,1,0:T(8,128)(2,1)S(1)}, u32[]{:S(2)}, u32[]{:S(2)}) async-start(bf16[16,16,2048]{2,1,0:T(8,128)(2,1)} %bitcast.10), calls=%async_computation.1 | async-start | bytes 2097152 | tf_op jit(solution)/shard_map/all_to_all | solution.py:50
  63.3 2.4 %gather_fusion = s32[256]{0:T(256)S(1)} fusion(s32[2,16,16]{2,1,0:T(8,128)S(1)} %sub.27, s32[256]{0:T(256)S(1)} %reshape.113), kind=kCustom, calls=%fused_computation.4 | custom fusion | bytes 5120 | tf_op jit(solution)/shard_map/jit(take_along_axis)/gather | solution.py:20
  66.3 2.8 %gather_fusion.4 = bf16[128,2048]{1,0:T(8,128)(2,1)S(1)} fusion(bf16[256,2048]{1,0:T(8,128)(2,1)} %bitcast.19, s32[1024]{0:T(1024)S(1)} %pad_clamp_fusion), kind=kCustom, calls=%fused_computation.3.clone | custom fusion | bytes 1049088 | tf_op jit(solution)/shard_map/jit(_take)/gather | solution.py:53
  69.1 17.0 %all-to-all-done.1 = bf16[16,16,2048]{2,1,0:T(8,128)(2,1)S(1)} async-done(((bf16[16,16,2048]{2,1,0:T(8,128)(2,1)}), bf16[16,16,2048]{2,1,0:T(8,128)(2,1)S(1)}, u32[]{:S(2)}, u32[]{:S(2)}) %all-to-all-start.1) | async-done | bytes 1048608 | tf_op jit(solution)/shard_map/all_to_all | solution.py:50
  86.1 0.9 %gather_fusion.2 = bf16[128,2048]{1,0:T(8,128)(2,1)S(1)} fusion(bf16[256,2048]{1,0:T(8,128)(2,1)S(1)} %bitcast.53, s32[1024]{0:T(1024)S(1)} %pad_clamp_fusion.2), kind=kCustom, calls=%fused_computation.1.clone | custom fusion | bytes 1049088 | tf_op jit(solution)/shard_map/jit(_take)/gather | solution.py:53
  87.0 1.1 %fusion.6 = f32[16,2048]{1,0:T(8,128)S(1)} fusion(bf16[128,2048]{1,0:T(8,128)(2,1)S(1)} %gather_fusion.4, f32[16,8]{1,0:T(8,128)S(1)} %copy.37, pred[128]{0:T(512)(128)(4,1)S(1)} %compare_and_fusion), kind=kLoop, calls=%fused_computation.14 | loop fusion | flops 1015808 | bytes 656000 | tf_op jit(solution)/shard_map/reduce_sum | solution.py:56
  88.1 1.1 %fusion.7 = f32[16,2048]{1,0:T(8,128)S(1)} fusion(bf16[128,2048]{1,0:T(8,128)(2,1)S(1)} %gather_fusion.2, f32[16,8]{1,0:T(8,128)S(1)} %copy.29, pred[128]{0:T(512)(128)(4,1)S(1)} %compare_and_fusion.2), kind=kLoop, calls=%fused_computation.16 | loop fusion | flops 1015808 | bytes 656000 | tf_op jit(solution)/shard_map/reduce_sum | solution.py:56
  (54 shorter events, 6.6 us)
Async XLA Ops:
  0.8 9.4 %copy-start.1 = (s32[2,16,8]{2,1,0:T(8,128)}, s32[2,16,8]{2,1,0:T(8,128)S(1)}, u32[]{:S(2)}) copy-start(s32[2,16,8]{2,1,0:T(8,128)S(1)} %copy.30) | copy-start | bytes 3076
  1.6 13.8 %all-to-all-start = ((s32[16,1,2]{2,1,0:T(1,128)}), s32[16,1,2]{2,1,0:T(1,128)S(1)}, u32[]{:S(2)}, u32[]{:S(2)}) async-start(s32[16,1,2]{2,1,0:T(1,128)} %copy.35), calls=%async_computation | async-start | bytes 16384 | tf_op jit(solution)/shard_map/all_to_all | solution.py:24
  26.5 10.7 %copy-start = (bf16[768,2048]{1,0:T(8,128)(2,1)S(1)}, bf16[768,2048]{1,0:T(8,128)(2,1)}, u32[]{:S(2)}) copy-start(bf16[768,2048]{1,0:T(8,128)(2,1)} %get-tuple-element.220) | copy-start | bytes 9437188
  29.1 27.3 %all-to-all-start.2 = ((bf16[16,16,2048]{2,1,0:T(8,128)(2,1)}), bf16[16,16,2048]{2,1,0:T(8,128)(2,1)}, u32[]{:S(2)}, u32[]{:S(2)}) async-start(bf16[16,16,2048]{2,1,0:T(8,128)(2,1)} %bitcast.54), calls=%async_computation.2 | async-start | bytes 2097152 | tf_op jit(solution)/shard_map/all_to_all | solution.py:50
  39.9 3.9 %copy-start.5 = (s32[256]{0:T(256)S(1)}, s32[256]{0:T(256)}, u32[]{:S(2)}) copy-start(s32[256]{0:T(256)} %min.15) | copy-start | bytes 3076
  43.8 19.3 %copy-start.2 = (s32[2,16,8]{2,1,0:T(8,128)S(1)}, s32[2,16,8]{2,1,0:T(8,128)}, u32[]{:S(2)}) copy-start(s32[2,16,8]{2,1,0:T(8,128)} %copy-done.1) | copy-start | bytes 3076
  56.3 29.8 %all-to-all-start.1 = ((bf16[16,16,2048]{2,1,0:T(8,128)(2,1)}), bf16[16,16,2048]{2,1,0:T(8,128)(2,1)S(1)}, u32[]{:S(2)}, u32[]{:S(2)}) async-start(bf16[16,16,2048]{2,1,0:T(8,128)(2,1)} %bitcast.10), calls=%async_computation.1 | async-start | bytes 2097152 | tf_op jit(solution)/shard_map/all_to_all | solution.py:50
  63.3 2.7 %copy-start.4 = (f32[2,16,8]{1,2,0:T(8,128)S(1)}, f32[2,16,8]{1,2,0:T(8,128)}, u32[]{:S(2)}) copy-start(f32[2,16,8]{1,2,0:T(8,128)} %param.16) | copy-start | bytes 3076
  69.1 20.1 %copy-start.3 = (bf16[2,16,2048]{2,1,0:T(8,128)(2,1)S(1)}, bf16[2,16,2048]{2,1,0:T(8,128)(2,1)}, u32[]{:S(2)}) copy-start(bf16[2,16,2048]{2,1,0:T(8,128)(2,1)} %param.17) | copy-start | bytes 393220
  69.1 20.1 %copy-start.6 = (bf16[2,16,2048]{2,1,0:T(8,128)(2,1)S(1)}, bf16[2,16,2048]{2,1,0:T(8,128)(2,1)}, u32[]{:S(2)}) copy-start(bf16[2,16,2048]{2,1,0:T(8,128)(2,1)} %custom-call.10) | copy-start | bytes 393220
  89.2 0.7 copy-start.7
where the time goes:
time: 90.9 us; the launch traced here: 89.9 us
  waiting for transfers between devices  33.5 us (37%)
  local copies, waits for them, and re-layouts  19.6 us (22%)
  starting transfers between devices  18.5 us (20%)
  other arithmetic  8.88 us (10%)
  matrix products  7.71 us (8%)
  between operations  1.63 us (2%)
    all_to_all x2, waiting for transfers between devices, shards(): lax.all_to_all(sending, 'ep', split_axis=0, concat_axis=0, tiled=True)  28.3 us
    all_to_all x2, starting transfers between devices, shards(): lax.all_to_all(sending, 'ep', split_axis=0, concat_axis=0, tiled=True)  11.1 us
    dot_general x4, matrix products, add_block(): jnp.dot(segment, matrix, preferred_element_type=jnp.float32)  7.71 us
    all_to_all x1, starting transfers between devices, shards(): lax.all_to_all(loads_out, 'ep', split_axis=0, concat_axis=0, tiled=True)  7.36 us
    gather x2, local copies, waits for them, and re-layouts, shards(): jnp.take(expert_produced, selector.reshape(-1), axis=0)  6.22 us
    all_to_all x1, waiting for transfers between devices, shards(): lax.all_to_all(loads_out, 'ep', split_axis=0, concat_axis=0, tiled=True)  5.17 us
    select_n x4, other arithmetic, shards(): jnp.take(expert_produced, selector.reshape(-1), axis=0)  4.4 us
    gather x2, local copies, waits for them, and re-layouts, shards(): jnp.take(flattened, location.reshape(-1), axis=0)  3.73 us
  transfers between devices with their start and end apart: 3, of which 3 were waited for; matrix products, arithmetic and copies ran while one was open for 21% of the time, Pallas kernels for 0%

commit v1 on v0

--- a/solution.py
+++ b/solution.py
@@ -1,8 +1,11 @@
+import functools
 import math
 
 import jax
 import jax.numpy as jnp
 from jax import lax
+from jax.experimental import pallas as pl
+from jax.experimental.pallas import tpu as pltpu
 from jax.sharding import PartitionSpec as P
 
 
@@ -60,7 +63,286 @@
     return jnp.stack(results, axis=0)
 
 
+MESH = pl.DeviceIdType.MESH
+TILE = 512
+
+
+def dense_kernel(
+    sizes, hidden_hbm, weight_hbm, routes_hbm, shares_hbm, residual_hbm, mixed_ref,
+    hidden, weight, routes, shares, residual, produced,
+    note_out, note_in, slot_of,
+    core_out, core_in, core_kept, x_out, x_in, x_kept, z_out, z_in,
+    load_sem, column_sem, note_send, note_recv, core_send, core_recv, x_send, x_recv, z_send, z_recv,
+):
+    ranks, batches, rows, chosen, slots, width = sizes
+    both = batches * rows
+    me = lax.axis_index("ep")
+    core, x, z = lax.rem(me, 2), lax.rem(me // 2, 2), me // 4
+    low, high = lax.rem(z, 2), z // 2
+    sibling = me + 1 - 2 * core
+    beside = me + 2 - 4 * x
+    near = me + 4 - 8 * low
+    far = me + 8 - 16 * high
+
+    barrier = pltpu.get_barrier_semaphore()
+
+    def greet(step, carry):
+        pl.semaphore_signal(
+            barrier, inc=1, device_id={"ep": lax.rem(me + step, ranks)}, device_id_type=MESH
+        )
+        return carry
+
+    lax.fori_loop(1, ranks, greet, 0)
+
+    loads = [
+        pltpu.make_async_copy(routes_hbm, routes, load_sem.at[0]),
+        pltpu.make_async_copy(shares_hbm, shares, load_sem.at[1]),
+        pltpu.make_async_copy(hidden_hbm, hidden, load_sem.at[2]),
+    ]
+    columns = [
+        pltpu.make_async_copy(
+            weight_hbm.at[:, pl.ds(j * TILE, TILE)], weight.at[j], column_sem.at[j]
+        )
+        for j in range(width // TILE)
+    ]
+    residual_load = pltpu.make_async_copy(residual_hbm, residual, load_sem.at[3])
+    for copy in loads + columns + [residual_load]:
+        copy.start()
+
+    loads[0].wait()
+    loads[1].wait()
+    expert = lax.broadcasted_iota(jnp.int32, (both, 128), 1)
+    given = jnp.zeros((both, 128), jnp.float32)
+    named = jnp.zeros((both, 128), jnp.float32)
+    route_rows, share_rows = routes[...], shares[...]
+    for k in range(chosen):
+        hit = route_rows[:, k : k + 1] == expert
+        given = given + jnp.where(hit, share_rows[:, k : k + 1], 0.0)
+        named = named + jnp.where(hit, 1.0, 0.0)
+    notes = jnp.concatenate(
+        [given, named, jnp.zeros((128 - 2 * both, 128), jnp.float32)], axis=0
+    )
+    notes = jnp.transpose(notes)[:ranks]
+    note_out[...] = notes.reshape(ranks, 1, 128)
+    note_in[pl.ds(me, 1)] = note_out[pl.ds(me, 1)]
+
+    pl.semaphore_wait(barrier, ranks - 1)
+
+    def note_to(step):
+        peer = lax.rem(me + step, ranks)
+        return pltpu.make_async_remote_copy(
+            src_ref=note_out.at[peer],
+            dst_ref=note_in.at[me],
+            send_sem=note_send.at[peer],
+            recv_sem=note_recv.at[me],
+            device_id={"ep": peer},
+            device_id_type=MESH,
+        )
+
+    def note_from(step):
+        peer = lax.rem(me + step, ranks)
+        return pltpu.make_async_remote_copy(
+            src_ref=note_out.at[peer],
+            dst_ref=note_in.at[peer],
+            send_sem=note_send.at[peer],
+            recv_sem=note_recv.at[peer],
+            device_id={"ep": peer},
+            device_id_type=MESH,
+        )
+
+    def send_note(step, carry):
+        note_to(step).start()
+        return carry
+
+    lax.fori_loop(1, ranks, send_note, 0)
+
+    loads[2].wait()
+    for j in range(width // TILE):
+        columns[j].wait()
+        for b in range(batches):
+            produced[b, :, j * TILE : (j + 1) * TILE] = jnp.dot(
+                hidden[b], weight[j], preferred_element_type=jnp.float32
+            ).astype(jnp.bfloat16)
+
+    def take_note(step, carry):
+        note_from(step).wait_recv()
+        return carry
+
+    lax.fori_loop(1, ranks, take_note, 0)
+
+    flags = note_in[...].reshape(ranks, 128)
+    upper = lax.broadcasted_iota(jnp.int32, (128, 128), 0)
+    lower = lax.broadcasted_iota(jnp.int32, (128, 128), 1)
+    alike = (upper >= both) & (upper < 2 * both) & (lower >= both) & (lower < 2 * both)
+    alike = alike & (upper // rows == lower // rows)
+    ones = jnp.where(alike, 1.0, 0.0).astype(jnp.bfloat16)
+    ahead = jnp.where(alike & (upper < lower), 1.0, 0.0).astype(jnp.bfloat16)
+    packed = flags.astype(jnp.bfloat16)
+    within = jnp.dot(packed, ahead, preferred_element_type=jnp.float32)
+    counts = jnp.dot(packed, ones, preferred_element_type=jnp.float32).astype(jnp.bfloat16)
+    earlier = lax.broadcasted_iota(jnp.int32, (ranks, ranks), 1) < lax.broadcasted_iota(
+        jnp.int32, (ranks, ranks), 0
+    )
+    before = jnp.dot(
+        jnp.where(earlier, 1.0, 0.0).astype(jnp.bfloat16), counts, preferred_element_type=jnp.float32
+    )
+    slot_of[...] = jnp.where(flags > 0.5, within + before, -1.0).reshape(ranks, 1, 128)
+
+    lane = lax.broadcasted_iota(jnp.int32, (both, 128), 1)
+    row = lax.broadcasted_iota(jnp.int32, (both, 128), 0)
+    slot = lax.broadcasted_iota(jnp.int32, (4 * rows, slots), 1).astype(jnp.float32)
+
+    def core_copy(i):
+        return pltpu.make_async_remote_copy(
+            src_ref=core_out.at[i], dst_ref=core_in.at[i],
+            send_sem=core_send.at[i], recv_sem=core_recv.at[i],
+            device_id={"ep": sibling}, device_id_type=MESH,
+        )
+
+    def x_copy(i):
+        return pltpu.make_async_remote_copy(
+            src_ref=x_out.at[i], dst_ref=x_in.at[i],
+            send_sem=x_send.at[i], recv_sem=x_recv.at[i],
+            device_id={"ep": beside}, device_id_type=MESH,
+        )
+
+    def z_copy(i):
+        return pltpu.make_async_remote_copy(
+            src_ref=z_out.at[i], dst_ref=z_in.at[i],
+            send_sem=z_send.at[i], recv_sem=z_recv.at[i],
+            device_id={"ep": far if i == 1 else near}, device_id_type=MESH,
+        )
+
+    def spread(i):
+        plane = 2 * lax.rem(high + 1 - i // 2, 2) + lax.rem(low + 1 - i % 2, 2)
+        factor, place = [], []
+        for other_core in (1, 0):
+            for other_x in (1, 0):
+                c = lax.rem(core + other_core, 2)
+                at_x = lax.rem(x + other_x, 2)
+                owner = plane * 4 + at_x * 2 + c
+                factor.append(
+                    jnp.sum(jnp.where(lane == row, note_in[owner], 0.0), axis=1, keepdims=True)
+                )
+                place.append(
+                    jnp.sum(jnp.where(lane == row + both, slot_of[owner], 0.0), axis=1, keepdims=True)
+                )
+        for b in range(batches):
+            span = slice(b * rows, (b + 1) * rows)
+            scale = jnp.concatenate([f[span] for f in factor], axis=0)
+            spot = jnp.concatenate([p[span] for p in place], axis=0)
+            pick = jnp.where(spot == slot, 1.0, 0.0).astype(jnp.bfloat16)
+            for j in range(width // TILE):
+                cut = slice(j * TILE, (j + 1) * TILE)
+                part = scale * jnp.dot(
+                    pick, produced[b, :, cut], preferred_element_type=jnp.float32
+                )
+                core_out[i, b, :, cut] = part[: 2 * rows].astype(jnp.bfloat16)
+                core_kept[i, b, :, cut] = part[2 * rows :]
+        core_copy(i).start()
+
+    def over_cores(i):
+        core_copy(i).wait_recv()
+        for b in range(batches):
+            total = core_kept[i, b] + core_in[i, b].astype(jnp.float32)
+            x_out[i, b] = total[:rows].astype(jnp.bfloat16)
+            x_kept[i, b] = total[rows:]
+        x_copy(i).start()
+
+    def over_x(i):
+        x_copy(i).wait_recv()
+        return x_kept[i] + x_in[i].astype(jnp.float32)
+
+    for i in range(4):
+        spread(i)
+        if i > 0:
+            over_cores(i - 1)
+    over_cores(3)
+
+    z_out[0] = over_x(0).astype(jnp.bfloat16)
+    z_copy(0).start()
+    total = over_x(1)
+    z_copy(0).wait_recv()
+    z_out[1] = (total + z_in[0].astype(jnp.float32)).astype(jnp.bfloat16)
+    z_copy(1).start()
+    z_out[2] = over_x(2).astype(jnp.bfloat16)
+    z_copy(2).start()
+    residual_load.wait()
+    total = over_x(3) + residual[...].astype(jnp.float32)
+    z_copy(1).wait_recv()
+    total = total + z_in[1].astype(jnp.float32)
+    z_copy(2).wait_recv()
+    mixed_ref[...] = (total + z_in[2].astype(jnp.float32)).astype(jnp.bfloat16)
+
+    for i in range(4):
+        core_copy(i).wait_send()
+        x_copy(i).wait_send()
+    for i in range(3):
+        z_copy(i).wait_send()
+
+    def note_left(step, carry):
+        note_to(step).wait_send()
+        return carry
+
+    lax.fori_loop(1, ranks, note_left, 0)
+
+
+def dense_shards(ranks, hidden, down_weight, routes, route_weight, residual):
+    batches, rows, chosen = routes.shape
+    slots, depth = hidden.shape[2:]
+    width = down_weight.shape[2]
+    both = batches * rows
+    bf16, f32 = jnp.bfloat16, jnp.float32
+    sizes = (ranks, batches, rows, chosen, slots, width)
+    parts = 4
+    return pl.pallas_call(
+        functools.partial(dense_kernel, sizes),
+        out_shape=jax.ShapeDtypeStruct((batches, rows, width), bf16),
+        in_specs=[pl.BlockSpec(memory_space=pl.ANY)] * 5,
+        out_specs=pl.BlockSpec(memory_space=pltpu.VMEM),
+        scratch_shapes=[
+            pltpu.VMEM((batches, slots, depth), bf16),
+            pltpu.VMEM((width // TILE, depth, TILE), bf16),
+            pltpu.VMEM((both, chosen), jnp.int32),
+            pltpu.VMEM((both, chosen), f32),
+            pltpu.VMEM((batches, rows, width), bf16),
+            pltpu.VMEM((batches, slots, width), bf16),
+            pltpu.VMEM((ranks, 1, 128), f32),
+            pltpu.VMEM((ranks, 1, 128), f32),
+            pltpu.VMEM((ranks, 1, 128), f32),
+            pltpu.VMEM((parts, batches, 2 * rows, width), bf16),
+            pltpu.VMEM((parts, batches, 2 * rows, width), bf16),
+            pltpu.VMEM((parts, batches, 2 * rows, width), f32),
+            pltpu.VMEM((parts, batches, rows, width), bf16),
+            pltpu.VMEM((parts, batches, rows, width), bf16),
+            pltpu.VMEM((parts, batches, rows, width), f32),
+            pltpu.VMEM((3, batches, rows, width), bf16),
+            pltpu.VMEM((3, batches, rows, width), bf16),
+            pltpu.SemaphoreType.DMA((4,)),
+            pltpu.SemaphoreType.DMA((width // TILE,)),
+            pltpu.SemaphoreType.DMA((ranks,)),
+            pltpu.SemaphoreType.DMA((ranks,)),
+            pltpu.SemaphoreType.DMA((parts,)),
+            pltpu.SemaphoreType.DMA((parts,)),
+            pltpu.SemaphoreType.DMA((parts,)),
+            pltpu.SemaphoreType.DMA((parts,)),
+            pltpu.SemaphoreType.DMA((3,)),
+            pltpu.SemaphoreType.DMA((3,)),
+        ],
+        compiler_params=pltpu.CompilerParams(
+            collective_id=0, has_side_effects=True, vmem_limit_bytes=48 * 1024 * 1024
+        ),
+    )(
+        hidden.reshape(batches, slots, depth),
+        down_weight.reshape(depth, width),
+        routes.reshape(both, chosen),
+        route_weight.reshape(both, chosen),
+        residual,
+    )
+
+
 def solution(mesh):
+    ranks = mesh.shape["ep"]
     in_specs = (
         P("dp", "ep", None, None),
         P("ep", None, None),
@@ -69,4 +351,15 @@
         P("dp", "ep", None),
     )
     out_specs = P("dp", "ep", None)
-    return jax.shard_map(shards, mesh=mesh, in_specs=in_specs, out_specs=out_specs, check_vma=False)
+
+    def run(hidden, down_weight, routes, route_weight, residual):
+        rows = routes.shape[1] // ranks
+        batches = routes.shape[0] // mesh.shape["dp"]
+        dense = ranks == 16 and rows % 16 == 0 and routes.shape[1] <= hidden.shape[2]
+        dense = dense and 2 * batches * rows <= 128
+        body = functools.partial(dense_shards, ranks) if dense else shards
+        return jax.shard_map(
+            body, mesh=mesh, in_specs=in_specs, out_specs=out_specs, check_vma=False
+        )(hidden, down_weight, routes, route_weight, residual)
+
+    return run

time: 90.9 us -> 36.5 us (0.40)
  waiting for transfers between devices: 33.5 us -> 0 us
  Pallas kernels: 0 us -> 30.1 us
  starting transfers between devices: 18.5 us -> 0 us
  local copies, waits for them, and re-layouts: 19.6 us -> 6.13 us
  other arithmetic: 8.88 us -> 0 us
  matrix products: 7.71 us -> 0 us
  between operations: 1.63 us -> 0.01 us
    all_to_all x3 -> x0, waiting for transfers between devices: 33.5 us -> none  [the longest x2 28.3 us: shards(): lax.all_to_all(sending, 'ep', split_axis=0, concat_axis=0, tiled=True)]
    pallas_call x0 -> x1, Pallas kernels: none -> 30.1 us  [dense_shards(): pl.pallas_call(functools.partial(dense_kernel, sizes), out_shape=jax.Shap...]
    all_to_all x3 -> x0, starting transfers between devices: 18.5 us -> none  [the longest x2 11.1 us: shards(): lax.all_to_all(sending, 'ep', split_axis=0, concat_axis=0, tiled=True)]
    gather x7 -> x0, local copies, waits for them, and re-layouts: 12.6 us -> none  [the longest x2 6.22 us: shards(): jnp.take(expert_produced, selector.reshape(-1), axis=0)]
    dot_general x4 -> x0, matrix products: 7.71 us -> none  [add_block(): jnp.dot(segment, matrix, preferred_element_type=jnp.float32)]
    unnamed x17 -> x9, local copies, waits for them, and re-layouts: 1.45 us -> 6.13 us
    select_n x7 -> x0, other arithmetic: 4.41 us -> none  [the longest x4 4.4 us: shards(): jnp.take(expert_produced, selector.reshape(-1), axis=0)]
    reduce_sum x4 -> x0, other arithmetic: 2.29 us -> none  [the longest x2 2.13 us: shards(): jnp.sum(route_weight[batch_index][:, :, None] * gathered.astype(jnp.float...]
  transfers between devices with their start and end apart: 3 -> 0, of which waited for: 3 -> 0; matrix products, arithmetic and copies ran while one was open for 21% -> 0% of each run, Pallas kernels for 0% -> 0%
where the time goes in v1:
time: 36.5 us; the launch traced here: 36.2 us
  Pallas kernels  30.1 us (82%)
  local copies, waits for them, and re-layouts  6.13 us (17%)
    pallas_call x1, Pallas kernels, dense_shards(): pl.pallas_call(functools.partial(dense_kernel, sizes), out_shape=jax.Shap...  30.1 us
    unnamed x9, local copies, waits for them, and re-layouts  6.13 us

profile of v1, /device:TPU:0, one launch (start us, length us, event | category | flops | bytes accessed | tf_op | source)
XLA Modules:
  0.0 36.2 jit_solution(5911214957914227884)
XLA Ops:
  0.0 0.8 %copy.6 = s32[2,16,8]{2,1,0:T(8,128)S(1)} copy(s32[2,16,8]{1,2,0:T(8,128)} %param.7) | data formatting | bytes 2048 | tf_op args[2]
  0.8 0.8 %copy.7 = f32[2,16,8]{2,1,0:T(8,128)S(1)} copy(f32[2,16,8]{1,2,0:T(8,128)} %param.8) | data formatting | bytes 2048 | tf_op args[3]
  1.5 0.0 copy-start
  1.5 1.9 %copy-done = bf16[1,768,2048]{2,1,0:T(8,128)(2,1)S(1)} copy-done((bf16[1,768,2048]{2,1,0:T(8,128)(2,1)S(1)}, bf16[1,768,2048]{2,1,0:T(8,128)(2,1)}, u32[]{:S(2)}) %copy-start) | copy-done | bytes 3145752
  3.4 0.0 copy-start.1
  3.4 1.1 %copy-done.1 = bf16[2,1,256,768]{3,2,1,0:T(8,128)(2,1)S(1)} copy-done((bf16[2,1,256,768]{3,2,1,0:T(8,128)(2,1)S(1)}, bf16[2,1,256,768]{3,2,1,0:T(8,128)(2,1)}, u32[]{:S(2)}) %copy-start.1) | copy-done | bytes 786456
  4.6 0.0 copy-start.2
  4.6 0.9 %copy-done.2 = bf16[2,16,2048]{2,1,0:T(8,128)(2,1)S(1)} copy-done((bf16[2,16,2048]{2,1,0:T(8,128)(2,1)S(1)}, bf16[2,16,2048]{2,1,0:T(8,128)(2,1)}, u32[]{:S(2)}) %copy-start.2) | copy-done | bytes 131096
  5.5 30.1 %shard_map.55 = bf16[2,16,2048]{2,1,0:T(8,128)(2,1)S(1)} custom-call(bf16[2,256,768]{2,1,0:T(8,128)(2,1)S(1)} %bitcast.5, bf16[768,2048]{1,0:T(8,128)(2,1)S(1)} %bitcast.4, s32[32,8]{1,0:T(8,128)S(1)} %bitcast.6, f32[32,8]{1,0:T(8,128)S(1)} %bitcast.7, bf16[2,16,2048]{2,1,0:T(8,128)(2,1)S(1)} %copy-done.2), custom_call_target="tpu_custom_call" | custom-call | tf_op jit(solution)/shard_map/pallas_call | solution.py:298
  35.5 0.7 %copy.9 = bf16[2,16,2048]{2,1,0:T(8,128)(2,1)} copy(bf16[2,16,2048]{2,1,0:T(8,128)(2,1)S(1)} %shard_map.55) | data formatting | bytes 262144
Async XLA Ops:
  1.5 1.9 %copy-start = (bf16[1,768,2048]{2,1,0:T(8,128)(2,1)S(1)}, bf16[1,768,2048]{2,1,0:T(8,128)(2,1)}, u32[]{:S(2)}) copy-start(bf16[1,768,2048]{2,1,0:T(8,128)(2,1)} %param.6) | copy-start | bytes 9437188
  3.4 1.1 %copy-start.1 = (bf16[2,1,256,768]{3,2,1,0:T(8,128)(2,1)S(1)}, bf16[2,1,256,768]{3,2,1,0:T(8,128)(2,1)}, u32[]{:S(2)}) copy-start(bf16[2,1,256,768]{3,2,1,0:T(8,128)(2,1)} %param.5) | copy-start | bytes 2359300
  4.6 0.9 %copy-start.2 = (bf16[2,16,2048]{2,1,0:T(8,128)(2,1)S(1)}, bf16[2,16,2048]{2,1,0:T(8,128)(2,1)}, u32[]{:S(2)}) copy-start(bf16[2,16,2048]{2,1,0:T(8,128)(2,1)} %residual_hbm.1) | copy-start | bytes 393220

commit v2 on v1

--- a/solution.py
+++ b/solution.py
@@ -111,18 +111,15 @@
 
     loads[0].wait()
     loads[1].wait()
-    expert = lax.broadcasted_iota(jnp.int32, (both, 128), 1)
-    given = jnp.zeros((both, 128), jnp.float32)
-    named = jnp.zeros((both, 128), jnp.float32)
-    route_rows, share_rows = routes[...], shares[...]
-    for k in range(chosen):
-        hit = route_rows[:, k : k + 1] == expert
-        given = given + jnp.where(hit, share_rows[:, k : k + 1], 0.0)
-        named = named + jnp.where(hit, 1.0, 0.0)
+    given, named = [], []
+    expert = lax.broadcasted_iota(jnp.int32, (ranks, chosen, rows), 0)
+    for b in range(batches):
+        hit = routes[b][None] == expert
+        given.append(jnp.sum(jnp.where(hit, shares[b][None], 0.0), axis=1))
+        named.append(jnp.sum(jnp.where(hit, 1.0, 0.0), axis=1))
     notes = jnp.concatenate(
-        [given, named, jnp.zeros((128 - 2 * both, 128), jnp.float32)], axis=0
-    )
-    notes = jnp.transpose(notes)[:ranks]
+        given + named + [jnp.zeros((ranks, 128 - 2 * both), jnp.float32)], axis=1
+    )
     note_out[...] = notes.reshape(ranks, 1, 128)
     note_in[pl.ds(me, 1)] = note_out[pl.ds(me, 1)]
 
@@ -303,8 +300,8 @@
         scratch_shapes=[
             pltpu.VMEM((batches, slots, depth), bf16),
             pltpu.VMEM((width // TILE, depth, TILE), bf16),
-            pltpu.VMEM((both, chosen), jnp.int32),
-            pltpu.VMEM((both, chosen), f32),
+            pltpu.VMEM((batches, chosen, rows), jnp.int32),
+            pltpu.VMEM((batches, chosen, rows), f32),
             pltpu.VMEM((batches, rows, width), bf16),
             pltpu.VMEM((batches, slots, width), bf16),
             pltpu.VMEM((ranks, 1, 128), f32),
@@ -330,13 +327,13 @@
             pltpu.SemaphoreType.DMA((3,)),
         ],
         compiler_params=pltpu.CompilerParams(
-            collective_id=0, has_side_effects=True, vmem_limit_bytes=48 * 1024 * 1024
+            collective_id=0, has_side_effects=True, vmem_limit_bytes=64 * 1024 * 1024
         ),
     )(
         hidden.reshape(batches, slots, depth),
         down_weight.reshape(depth, width),
-        routes.reshape(both, chosen),
-        route_weight.reshape(both, chosen),
+        jnp.swapaxes(routes, 1, 2),
+        jnp.swapaxes(route_weight, 1, 2),
         residual,
     )
 

time: 36.5 us -> 32.5 us (0.89)
  local copies, waits for them, and re-layouts: 6.13 us -> 1.57 us
  Pallas kernels: 30.1 us -> 30.7 us
    unnamed x9 -> x1, local copies, waits for them, and re-layouts: 6.13 us -> 1.57 us
    pallas_call x1, Pallas kernels: 30.1 us -> 30.7 us  [dense_shards(): pl.pallas_call(functools.partial(dense_kernel, sizes), out_shape=jax.Shap...]
where the time goes in v2:
time: 32.5 us; the launch traced here: 32.3 us
  Pallas kernels  30.7 us (94%)
  local copies, waits for them, and re-layouts  1.57 us (5%)
    pallas_call x1, Pallas kernels, dense_shards(): pl.pallas_call(functools.partial(dense_kernel, sizes), out_shape=jax.Shap...  30.7 us
    unnamed x1, local copies, waits for them, and re-layouts  1.57 us

profile of v2, /device:TPU:0, one launch (start us, length us, event | category | flops | bytes accessed | tf_op | source)
XLA Modules:
  0.0 32.3 jit_solution(4748616398988456381)
XLA Ops:
  0.0 30.7 %shard_map.55 = bf16[2,16,2048]{2,1,0:T(8,128)(2,1)} custom-call(bf16[2,256,768]{2,1,0:T(8,128)(2,1)} %bitcast.5, bf16[768,2048]{1,0:T(8,128)(2,1)} %bitcast.4, s32[2,8,16]{2,1,0:T(8,128)} %bitcast.6, f32[2,8,16]{2,1,0:T(8,128)} %bitcast.7, bf16[2,16,2048]{2,1,0:T(8,128)(2,1)} %residual_hbm.1), custom_call_target="tpu_custom_call" | custom-call | tf_op jit(solution)/shard_map/pallas_call | solution.py:295
  30.7 1.6 %copy.7 = bf16[2,16,2048]{2,1,0:T(8,128)(2,1)} copy(bf16[2,16,2048]{2,1,0:T(8,128)(2,1)} %shard_map.55) | data formatting | bytes 262144

commit v3 on v2

--- a/solution.py
+++ b/solution.py
@@ -153,13 +153,17 @@
 
     lax.fori_loop(1, ranks, send_note, 0)
 
-    loads[2].wait()
-    for j in range(width // TILE):
-        columns[j].wait()
-        for b in range(batches):
+    def produce(b, tiles):
+        for j in tiles:
+            if b == 0:
+                columns[j].wait()
             produced[b, :, j * TILE : (j + 1) * TILE] = jnp.dot(
                 hidden[b], weight[j], preferred_element_type=jnp.float32
             ).astype(jnp.bfloat16)
+
+    tiles = width // TILE
+    loads[2].wait()
+    produce(0, range(tiles))
 
     def take_note(step, carry):
         note_from(step).wait_recv()
@@ -185,32 +189,32 @@
     )
     slot_of[...] = jnp.where(flags > 0.5, within + before, -1.0).reshape(ranks, 1, 128)
 
-    lane = lax.broadcasted_iota(jnp.int32, (both, 128), 1)
-    row = lax.broadcasted_iota(jnp.int32, (both, 128), 0)
+    lane = lax.broadcasted_iota(jnp.int32, (rows, 128), 1)
+    row = lax.broadcasted_iota(jnp.int32, (rows, 128), 0)
     slot = lax.broadcasted_iota(jnp.int32, (4 * rows, slots), 1).astype(jnp.float32)
 
-    def core_copy(i):
-        return pltpu.make_async_remote_copy(
-            src_ref=core_out.at[i], dst_ref=core_in.at[i],
-            send_sem=core_send.at[i], recv_sem=core_recv.at[i],
+    def core_copy(i, b):
+        return pltpu.make_async_remote_copy(
+            src_ref=core_out.at[i, b], dst_ref=core_in.at[i, b],
+            send_sem=core_send.at[i, b], recv_sem=core_recv.at[i, b],
             device_id={"ep": sibling}, device_id_type=MESH,
         )
 
-    def x_copy(i):
-        return pltpu.make_async_remote_copy(
-            src_ref=x_out.at[i], dst_ref=x_in.at[i],
-            send_sem=x_send.at[i], recv_sem=x_recv.at[i],
+    def x_copy(i, b):
+        return pltpu.make_async_remote_copy(
+            src_ref=x_out.at[i, b], dst_ref=x_in.at[i, b],
+            send_sem=x_send.at[i, b], recv_sem=x_recv.at[i, b],
             device_id={"ep": beside}, device_id_type=MESH,
         )
 
-    def z_copy(i):
-        return pltpu.make_async_remote_copy(
-            src_ref=z_out.at[i], dst_ref=z_in.at[i],
-            send_sem=z_send.at[i], recv_sem=z_recv.at[i],
+    def z_copy(i, b):
+        return pltpu.make_async_remote_copy(
+            src_ref=z_out.at[i, b], dst_ref=z_in.at[i, b],
+            send_sem=z_send.at[i, b], recv_sem=z_recv.at[i, b],
             device_id={"ep": far if i == 1 else near}, device_id_type=MESH,
         )
 
-    def spread(i):
+    def spread(i, b):
         plane = 2 * lax.rem(high + 1 - i // 2, 2) + lax.rem(low + 1 - i % 2, 2)
         factor, place = [], []
         for other_core in (1, 0):
@@ -219,63 +223,80 @@
                 at_x = lax.rem(x + other_x, 2)
                 owner = plane * 4 + at_x * 2 + c
                 factor.append(
-                    jnp.sum(jnp.where(lane == row, note_in[owner], 0.0), axis=1, keepdims=True)
+                    jnp.sum(
+                        jnp.where(lane == row + b * rows, note_in[owner], 0.0), axis=1, keepdims=True
+                    )
                 )
                 place.append(
-                    jnp.sum(jnp.where(lane == row + both, slot_of[owner], 0.0), axis=1, keepdims=True)
+                    jnp.sum(
+                        jnp.where(lane == row + (both + b * rows), slot_of[owner], 0.0),
+                        axis=1, keepdims=True,
+                    )
                 )
-        for b in range(batches):
-            span = slice(b * rows, (b + 1) * rows)
-            scale = jnp.concatenate([f[span] for f in factor], axis=0)
-            spot = jnp.concatenate([p[span] for p in place], axis=0)
-            pick = jnp.where(spot == slot, 1.0, 0.0).astype(jnp.bfloat16)
-            for j in range(width // TILE):
-                cut = slice(j * TILE, (j + 1) * TILE)
-                part = scale * jnp.dot(
-                    pick, produced[b, :, cut], preferred_element_type=jnp.float32
-                )
-                core_out[i, b, :, cut] = part[: 2 * rows].astype(jnp.bfloat16)
-                core_kept[i, b, :, cut] = part[2 * rows :]
-        core_copy(i).start()
-
-    def over_cores(i):
-        core_copy(i).wait_recv()
-        for b in range(batches):
-            total = core_kept[i, b] + core_in[i, b].astype(jnp.float32)
-            x_out[i, b] = total[:rows].astype(jnp.bfloat16)
-            x_kept[i, b] = total[rows:]
-        x_copy(i).start()
-
-    def over_x(i):
-        x_copy(i).wait_recv()
-        return x_kept[i] + x_in[i].astype(jnp.float32)
-
-    for i in range(4):
-        spread(i)
-        if i > 0:
-            over_cores(i - 1)
-    over_cores(3)
-
-    z_out[0] = over_x(0).astype(jnp.bfloat16)
-    z_copy(0).start()
-    total = over_x(1)
-    z_copy(0).wait_recv()
-    z_out[1] = (total + z_in[0].astype(jnp.float32)).astype(jnp.bfloat16)
-    z_copy(1).start()
-    z_out[2] = over_x(2).astype(jnp.bfloat16)
-    z_copy(2).start()
+        scale = jnp.concatenate(factor, axis=0)
+        spot = jnp.concatenate(place, axis=0)
+        pick = jnp.where(spot == slot, 1.0, 0.0).astype(jnp.bfloat16)
+        for j in range(tiles):
+            cut = slice(j * TILE, (j + 1) * TILE)
+            part = scale * jnp.dot(pick, produced[b, :, cut], preferred_element_type=jnp.float32)
+            core_out[i, b, :, cut] = part[: 2 * rows].astype(jnp.bfloat16)
+            core_kept[i, b, :, cut] = part[2 * rows :]
+        core_copy(i, b).start()
+
+    def over_cores(i, b):
+        core_copy(i, b).wait_recv()
+        total = core_kept[i, b] + core_in[i, b].astype(jnp.float32)
+        x_out[i, b] = total[:rows].astype(jnp.bfloat16)
+        x_kept[i, b] = total[rows:]
+        x_copy(i, b).start()
+
+    def over_x(i, b):
+        x_copy(i, b).wait_recv()
+        total = x_kept[i, b] + x_in[i, b].astype(jnp.float32)
+        if i == 1:
+            z_copy(0, b).wait_recv()
+            total = total + z_in[0, b].astype(jnp.float32)
+        if i < 3:
+            z_out[i, b] = total.astype(jnp.bfloat16)
+            z_copy(i, b).start()
+        else:
+            total = total + residual[b].astype(jnp.float32)
+            z_copy(2, b).wait_recv()
+            total = total + z_in[2, b].astype(jnp.float32)
+            z_copy(1, b).wait_recv()
+            mixed_ref[b] = (total + z_in[1, b].astype(jnp.float32)).astype(jnp.bfloat16)
+
+    order = [(0, 0), (1, 0), (0, 1), (1, 1), (2, 0), (2, 1), (3, 0), (3, 1)]
+    spread(*order[0])
+    spread(*order[1])
+    over_cores(*order[0])
+    produce(1, range(tiles // 2))
+    over_cores(*order[1])
+    produce(1, range(tiles // 2, tiles))
+    spread(*order[2])
+    over_x(*order[0])
+    spread(*order[3])
+    over_cores(*order[2])
+    spread(*order[4])
+    over_cores(*order[3])
+    over_x(*order[1])
+    spread(*order[5])
+    over_cores(*order[4])
+    spread(*order[6])
+    over_cores(*order[5])
+    over_x(*order[2])
+    spread(*order[7])
+    over_cores(*order[6])
+    over_cores(*order[7])
     residual_load.wait()
-    total = over_x(3) + residual[...].astype(jnp.float32)
-    z_copy(1).wait_recv()
-    total = total + z_in[1].astype(jnp.float32)
-    z_copy(2).wait_recv()
-    mixed_ref[...] = (total + z_in[2].astype(jnp.float32)).astype(jnp.bfloat16)
-
-    for i in range(4):
-        core_copy(i).wait_send()
-        x_copy(i).wait_send()
-    for i in range(3):
-        z_copy(i).wait_send()
+    for part in order[3:]:
+        over_x(*part)
+
+    for part in order:
+        core_copy(*part).wait_send()
+        x_copy(*part).wait_send()
+        if part[0] < 3:
+            z_copy(*part).wait_send()
 
     def note_left(step, carry):
         note_to(step).wait_send()
@@ -319,15 +340,15 @@
             pltpu.SemaphoreType.DMA((width // TILE,)),
             pltpu.SemaphoreType.DMA((ranks,)),
             pltpu.SemaphoreType.DMA((ranks,)),
-            pltpu.SemaphoreType.DMA((parts,)),
-            pltpu.SemaphoreType.DMA((parts,)),
-            pltpu.SemaphoreType.DMA((parts,)),
-            pltpu.SemaphoreType.DMA((parts,)),
-            pltpu.SemaphoreType.DMA((3,)),
-            pltpu.SemaphoreType.DMA((3,)),
+            pltpu.SemaphoreType.DMA((parts, batches)),
+            pltpu.SemaphoreType.DMA((parts, batches)),
+            pltpu.SemaphoreType.DMA((parts, batches)),
+            pltpu.SemaphoreType.DMA((parts, batches)),
+            pltpu.SemaphoreType.DMA((3, batches)),
+            pltpu.SemaphoreType.DMA((3, batches)),
         ],
         compiler_params=pltpu.CompilerParams(
-            collective_id=0, has_side_effects=True, vmem_limit_bytes=64 * 1024 * 1024
+            collective_id=0, has_side_effects=True, vmem_limit_bytes=64 * 1024 * 1024 - 132 * 1024
         ),
     )(
         hidden.reshape(batches, slots, depth),
@@ -353,7 +374,7 @@
         rows = routes.shape[1] // ranks
         batches = routes.shape[0] // mesh.shape["dp"]
         dense = ranks == 16 and rows % 16 == 0 and routes.shape[1] <= hidden.shape[2]
-        dense = dense and 2 * batches * rows <= 128
+        dense = dense and batches == 2 and 2 * batches * rows <= 128
         body = functools.partial(dense_shards, ranks) if dense else shards
         return jax.shard_map(
             body, mesh=mesh, in_specs=in_specs, out_specs=out_specs, check_vma=False

time: 32.5 us -> 32.1 us (0.988)
  Pallas kernels: 30.7 us -> 30.3 us
    pallas_call x1, Pallas kernels: 30.7 us -> 30.3 us  [dense_shards(): pl.pallas_call(functools.partial(dense_kernel, sizes), out_shape=jax.Shap...]
where the time goes in v3:
time: 32.1 us; the launch traced here: 31.9 us
  Pallas kernels  30.3 us (94%)
  local copies, waits for them, and re-layouts  1.57 us (5%)
    pallas_call x1, Pallas kernels, dense_shards(): pl.pallas_call(functools.partial(dense_kernel, sizes), out_shape=jax.Shap...  30.3 us
    unnamed x1, local copies, waits for them, and re-layouts  1.57 us

profile of v3, /device:TPU:0, one launch (start us, length us, event | category | flops | bytes accessed | tf_op | source)
XLA Modules:
  0.0 31.9 jit_solution(15702146883776494133)
XLA Ops:
  0.0 30.3 %shard_map.55 = bf16[2,16,2048]{2,1,0:T(8,128)(2,1)} custom-call(bf16[2,256,768]{2,1,0:T(8,128)(2,1)} %bitcast.5, bf16[768,2048]{1,0:T(8,128)(2,1)} %bitcast.4, s32[2,8,16]{2,1,0:T(8,128)} %bitcast.6, f32[2,8,16]{2,1,0:T(8,128)} %bitcast.7, bf16[2,16,2048]{2,1,0:T(8,128)(2,1)} %residual_hbm.1), custom_call_target="tpu_custom_call" | custom-call | tf_op jit(solution)/shard_map/pallas_call | solution.py:316
  30.3 1.6 %copy.7 = bf16[2,16,2048]{2,1,0:T(8,128)(2,1)} copy(bf16[2,16,2048]{2,1,0:T(8,128)(2,1)} %shard_map.55) | data formatting | bytes 262144

commit v4 on v3

--- a/solution.py
+++ b/solution.py
@@ -191,7 +191,7 @@
 
     lane = lax.broadcasted_iota(jnp.int32, (rows, 128), 1)
     row = lax.broadcasted_iota(jnp.int32, (rows, 128), 0)
-    slot = lax.broadcasted_iota(jnp.int32, (4 * rows, slots), 1).astype(jnp.float32)
+    slot = lax.broadcasted_iota(jnp.int32, (8 * rows, slots), 1).astype(jnp.float32)
 
     def core_copy(i, b):
         return pltpu.make_async_remote_copy(
@@ -214,34 +214,36 @@
             device_id={"ep": far if i == 1 else near}, device_id_type=MESH,
         )
 
-    def spread(i, b):
-        plane = 2 * lax.rem(high + 1 - i // 2, 2) + lax.rem(low + 1 - i % 2, 2)
+    def spread(parts, b):
         factor, place = [], []
-        for other_core in (1, 0):
-            for other_x in (1, 0):
-                c = lax.rem(core + other_core, 2)
-                at_x = lax.rem(x + other_x, 2)
-                owner = plane * 4 + at_x * 2 + c
-                factor.append(
-                    jnp.sum(
-                        jnp.where(lane == row + b * rows, note_in[owner], 0.0), axis=1, keepdims=True
+        for i in parts:
+            plane = 2 * lax.rem(high + 1 - i // 2, 2) + lax.rem(low + 1 - i % 2, 2)
+            for other_core in (1, 0):
+                for other_x in (1, 0):
+                    c = lax.rem(core + other_core, 2)
+                    at_x = lax.rem(x + other_x, 2)
+                    owner = plane * 4 + at_x * 2 + c
+                    note, spot = note_in[owner], slot_of[owner]
+                    factor.append(
+                        jnp.sum(jnp.where(lane == row + b * rows, note, 0.0), axis=1, keepdims=True)
                     )
-                )
-                place.append(
-                    jnp.sum(
-                        jnp.where(lane == row + (both + b * rows), slot_of[owner], 0.0),
-                        axis=1, keepdims=True,
+                    place.append(
+                        jnp.sum(
+                            jnp.where(lane == row + (both + b * rows), spot, 0.0),
+                            axis=1, keepdims=True,
+                        )
                     )
-                )
         scale = jnp.concatenate(factor, axis=0)
-        spot = jnp.concatenate(place, axis=0)
-        pick = jnp.where(spot == slot, 1.0, 0.0).astype(jnp.bfloat16)
+        pick = jnp.where(jnp.concatenate(place, axis=0) == slot, 1.0, 0.0).astype(jnp.bfloat16)
         for j in range(tiles):
             cut = slice(j * TILE, (j + 1) * TILE)
             part = scale * jnp.dot(pick, produced[b, :, cut], preferred_element_type=jnp.float32)
-            core_out[i, b, :, cut] = part[: 2 * rows].astype(jnp.bfloat16)
-            core_kept[i, b, :, cut] = part[2 * rows :]
-        core_copy(i, b).start()
+            for step, i in enumerate(parts):
+                top = 4 * rows * step
+                core_out[i, b, :, cut] = part[top : top + 2 * rows].astype(jnp.bfloat16)
+                core_kept[i, b, :, cut] = part[top + 2 * rows : top + 4 * rows]
+        for i in parts:
+            core_copy(i, b).start()
 
     def over_cores(i, b):
         core_copy(i, b).wait_recv()
@@ -267,29 +269,24 @@
             mixed_ref[b] = (total + z_in[1, b].astype(jnp.float32)).astype(jnp.bfloat16)
 
     order = [(0, 0), (1, 0), (0, 1), (1, 1), (2, 0), (2, 1), (3, 0), (3, 1)]
-    spread(*order[0])
-    spread(*order[1])
-    over_cores(*order[0])
+    spread((0, 1), 0)
     produce(1, range(tiles // 2))
-    over_cores(*order[1])
+    over_cores(0, 0)
+    over_cores(1, 0)
     produce(1, range(tiles // 2, tiles))
-    spread(*order[2])
-    over_x(*order[0])
-    spread(*order[3])
-    over_cores(*order[2])
-    spread(*order[4])
-    over_cores(*order[3])
-    over_x(*order[1])
-    spread(*order[5])
-    over_cores(*order[4])
-    spread(*order[6])
-    over_cores(*order[5])
-    over_x(*order[2])
-    spread(*order[7])
-    over_cores(*order[6])
-    over_cores(*order[7])
+    spread((0, 1), 1)
+    over_x(0, 0)
+    spread((2, 3), 0)
+    over_cores(0, 1)
+    over_cores(1, 1)
+    over_x(1, 0)
+    spread((2, 3), 1)
+    over_cores(2, 0)
+    over_cores(2, 1)
+    over_cores(3, 0)
+    over_cores(3, 1)
     residual_load.wait()
-    for part in order[3:]:
+    for part in order[2:]:
         over_x(*part)
 
     for part in order:
@@ -348,14 +345,19 @@
             pltpu.SemaphoreType.DMA((3, batches)),
         ],
         compiler_params=pltpu.CompilerParams(
-            collective_id=0, has_side_effects=True, vmem_limit_bytes=64 * 1024 * 1024 - 132 * 1024
+            collective_id=0, has_side_effects=True, vmem_limit_bytes=48 * 1024 * 1024
         ),
     )(
-        hidden.reshape(batches, slots, depth),
-        down_weight.reshape(depth, width),
-        jnp.swapaxes(routes, 1, 2),
-        jnp.swapaxes(route_weight, 1, 2),
-        residual,
+        *[
+            pltpu.with_memory_space_constraint(operand, pltpu.HBM)
+            for operand in (
+                hidden.reshape(batches, slots, depth),
+                down_weight.reshape(depth, width),
+                jnp.swapaxes(routes, 1, 2),
+                jnp.swapaxes(route_weight, 1, 2),
+                residual,
+            )
+        ]
     )
 
 

time: 32.1 us -> 30.7 us (0.956)
  local copies, waits for them, and re-layouts: 1.57 us -> 0.66 us
  Pallas kernels: 30.3 us -> 29.9 us
    unnamed x1, local copies, waits for them, and re-layouts: 1.57 us -> 0.66 us
    pallas_call x1, Pallas kernels: 30.3 us -> 29.9 us  [dense_shards(): pl.pallas_call(functools.partial(dense_kernel, sizes), out_shape=jax.Shap...]
where the time goes in v4:
time: 30.7 us; the launch traced here: 30.5 us
  Pallas kernels  29.9 us (97%)
  local copies, waits for them, and re-layouts  0.66 us (2%)
    pallas_call x1, Pallas kernels, dense_shards(): pl.pallas_call(functools.partial(dense_kernel, sizes), out_shape=jax.Shap...  29.9 us
    unnamed x1, local copies, waits for them, and re-layouts  0.66 us

profile of v4, /device:TPU:0, one launch (start us, length us, event | category | flops | bytes accessed | tf_op | source)
XLA Modules:
  0.0 30.5 jit_solution(2882599829795937226)
XLA Ops:
  0.0 29.9 %shard_map.55 = bf16[2,16,2048]{2,1,0:T(8,128)(2,1)S(1)} custom-call(bf16[2,256,768]{2,1,0:T(8,128)(2,1)} %bitcast.5, bf16[768,2048]{1,0:T(8,128)(2,1)} %bitcast.4, s32[2,8,16]{2,1,0:T(8,128)} %bitcast.6, f32[2,8,16]{2,1,0:T(8,128)} %bitcast.7, bf16[2,16,2048]{2,1,0:T(8,128)(2,1)} %residual_hbm.1), custom_call_target="tpu_custom_call" | custom-call | tf_op jit(solution)/shard_map/pallas_call | solution.py:313
  29.9 0.7 %copy.7 = bf16[2,16,2048]{2,1,0:T(8,128)(2,1)} copy(bf16[2,16,2048]{2,1,0:T(8,128)(2,1)S(1)} %shard_map.55) | data formatting | bytes 262144

commit v5 on v4

--- a/solution.py
+++ b/solution.py
@@ -250,12 +250,14 @@
         total = core_kept[i, b] + core_in[i, b].astype(jnp.float32)
         x_out[i, b] = total[:rows].astype(jnp.bfloat16)
         x_kept[i, b] = total[rows:]
-        x_copy(i, b).start()
-
-    def over_x(i, b):
+
+    def over_x(at):
+        i, b = order[at]
         x_copy(i, b).wait_recv()
         total = x_kept[i, b] + x_in[i, b].astype(jnp.float32)
         if i == 1:
+            if at + 2 < len(order):
+                x_copy(*order[at + 2]).start()
             z_copy(0, b).wait_recv()
             total = total + z_in[0, b].astype(jnp.float32)
         if i < 3:
@@ -267,27 +269,32 @@
             total = total + z_in[2, b].astype(jnp.float32)
             z_copy(1, b).wait_recv()
             mixed_ref[b] = (total + z_in[1, b].astype(jnp.float32)).astype(jnp.bfloat16)
+        if i != 1 and at + 2 < len(order):
+            x_copy(*order[at + 2]).start()
 
     order = [(0, 0), (1, 0), (0, 1), (1, 1), (2, 0), (2, 1), (3, 0), (3, 1)]
     spread((0, 1), 0)
     produce(1, range(tiles // 2))
     over_cores(0, 0)
+    x_copy(0, 0).start()
     over_cores(1, 0)
+    x_copy(1, 0).start()
     produce(1, range(tiles // 2, tiles))
     spread((0, 1), 1)
-    over_x(0, 0)
+    over_cores(0, 1)
+    over_x(0)
+    over_cores(1, 1)
     spread((2, 3), 0)
-    over_cores(0, 1)
-    over_cores(1, 1)
-    over_x(1, 0)
+    over_x(1)
     spread((2, 3), 1)
     over_cores(2, 0)
     over_cores(2, 1)
+    over_x(2)
     over_cores(3, 0)
     over_cores(3, 1)
     residual_load.wait()
-    for part in order[2:]:
-        over_x(*part)
+    for at in range(3, len(order)):
+        over_x(at)
 
     for part in order:
         core_copy(*part).wait_send()

time: 30.7 us -> 30.6 us (level)
  no operation moved by 1% of the time
where the time goes in v5:
time: 30.6 us; the launch traced here: 30.4 us
  Pallas kernels  29.7 us (97%)
  local copies, waits for them, and re-layouts  0.66 us (2%)
    pallas_call x1, Pallas kernels, dense_shards(): pl.pallas_call(functools.partial(dense_kernel, sizes), out_shape=jax.Shap...  29.7 us
    unnamed x1, local copies, waits for them, and re-layouts  0.66 us

profile of v5, /device:TPU:0, one launch (start us, length us, event | category | flops | bytes accessed | tf_op | source)
XLA Modules:
  0.0 30.4 jit_solution(15743112858541225750)
XLA Ops:
  0.0 29.7 %shard_map.55 = bf16[2,16,2048]{2,1,0:T(8,128)(2,1)S(1)} custom-call(bf16[2,256,768]{2,1,0:T(8,128)(2,1)} %bitcast.5, bf16[768,2048]{1,0:T(8,128)(2,1)} %bitcast.4, s32[2,8,16]{2,1,0:T(8,128)} %bitcast.6, f32[2,8,16]{2,1,0:T(8,128)} %bitcast.7, bf16[2,16,2048]{2,1,0:T(8,128)(2,1)} %residual_hbm.1), custom_call_target="tpu_custom_call" | custom-call | tf_op jit(solution)/shard_map/pallas_call | solution.py:320
  29.7 0.7 %copy.7 = bf16[2,16,2048]{2,1,0:T(8,128)(2,1)} copy(bf16[2,16,2048]{2,1,0:T(8,128)(2,1)S(1)} %shard_map.55) | data formatting | bytes 262144

commit v6 on v4

--- a/solution.py
+++ b/solution.py
@@ -71,8 +71,9 @@
     sizes, hidden_hbm, weight_hbm, routes_hbm, shares_hbm, residual_hbm, mixed_ref,
     hidden, weight, routes, shares, residual, produced,
     note_out, note_in, slot_of,
-    core_out, core_in, core_kept, x_out, x_in, x_kept, z_out, z_in,
+    core_out, core_in, core_kept, x_out, x_in, x_kept, z_out, z_in, near_out, near_in, near_kept,
     load_sem, column_sem, note_send, note_recv, core_send, core_recv, x_send, x_recv, z_send, z_recv,
+    near_send, near_recv,
 ):
     ranks, batches, rows, chosen, slots, width = sizes
     both = batches * rows
@@ -164,6 +165,7 @@
     tiles = width // TILE
     loads[2].wait()
     produce(0, range(tiles))
+    produce(1, range(tiles))
 
     def take_note(step, carry):
         note_from(step).wait_recv()
@@ -245,17 +247,37 @@
         for i in parts:
             core_copy(i, b).start()
 
+    def near_copy(k):
+        return pltpu.make_async_remote_copy(
+            src_ref=near_out.at[k], dst_ref=near_in.at[k],
+            send_sem=near_send.at[k], recv_sem=near_recv.at[k],
+            device_id={"ep": near}, device_id_type=MESH,
+        )
+
     def over_cores(i, b):
         core_copy(i, b).wait_recv()
         total = core_kept[i, b] + core_in[i, b].astype(jnp.float32)
-        x_out[i, b] = total[:rows].astype(jnp.bfloat16)
-        x_kept[i, b] = total[rows:]
-        x_copy(i, b).start()
+        if b == 0:
+            x_out[i, b] = total[:rows].astype(jnp.bfloat16)
+            x_kept[i, b] = total[rows:]
+            x_copy(i, b).start()
+        elif i % 2 == 0:
+            near_out[i // 2] = total.astype(jnp.bfloat16)
+            near_copy(i // 2).start()
+        else:
+            near_kept[i // 2] = total
+
+    def over_near(i):
+        near_copy(i // 2).wait_recv()
+        total = near_kept[i // 2] + near_in[i // 2].astype(jnp.float32)
+        x_out[i, 1] = total[:rows].astype(jnp.bfloat16)
+        x_kept[i, 1] = total[rows:]
+        x_copy(i, 1).start()
 
     def over_x(i, b):
         x_copy(i, b).wait_recv()
         total = x_kept[i, b] + x_in[i, b].astype(jnp.float32)
-        if i == 1:
+        if i == 1 and b == 0:
             z_copy(0, b).wait_recv()
             total = total + z_in[0, b].astype(jnp.float32)
         if i < 3:
@@ -263,37 +285,44 @@
             z_copy(i, b).start()
         else:
             total = total + residual[b].astype(jnp.float32)
-            z_copy(2, b).wait_recv()
-            total = total + z_in[2, b].astype(jnp.float32)
+            if b == 0:
+                z_copy(2, b).wait_recv()
+                total = total + z_in[2, b].astype(jnp.float32)
             z_copy(1, b).wait_recv()
             mixed_ref[b] = (total + z_in[1, b].astype(jnp.float32)).astype(jnp.bfloat16)
 
-    order = [(0, 0), (1, 0), (0, 1), (1, 1), (2, 0), (2, 1), (3, 0), (3, 1)]
     spread((0, 1), 0)
-    produce(1, range(tiles // 2))
+    spread((0, 1), 1)
     over_cores(0, 0)
+    over_cores(0, 1)
     over_cores(1, 0)
-    produce(1, range(tiles // 2, tiles))
-    spread((0, 1), 1)
+    over_cores(1, 1)
+    spread((2, 3), 0)
+    over_cores(2, 0)
     over_x(0, 0)
-    spread((2, 3), 0)
-    over_cores(0, 1)
-    over_cores(1, 1)
+    over_cores(3, 0)
+    spread((2, 3), 1)
+    over_near(1)
+    over_cores(2, 1)
+    over_cores(3, 1)
     over_x(1, 0)
-    spread((2, 3), 1)
-    over_cores(2, 0)
-    over_cores(2, 1)
-    over_cores(3, 0)
-    over_cores(3, 1)
+    over_x(2, 0)
+    over_x(1, 1)
+    over_near(3)
     residual_load.wait()
-    for part in order[2:]:
-        over_x(*part)
-
-    for part in order:
-        core_copy(*part).wait_send()
-        x_copy(*part).wait_send()
-        if part[0] < 3:
-            z_copy(*part).wait_send()
+    over_x(3, 0)
+    over_x(3, 1)
+
+    for i in range(4):
+        for b in range(batches):
+            core_copy(i, b).wait_send()
+        x_copy(i, 0).wait_send()
+    for k in range(2):
+        near_copy(k).wait_send()
+        x_copy(2 * k + 1, 1).wait_send()
+    for i in range(3):
+        z_copy(i, 0).wait_send()
+    z_copy(1, 1).wait_send()
 
     def note_left(step, carry):
         note_to(step).wait_send()
@@ -333,6 +362,9 @@
             pltpu.VMEM((parts, batches, rows, width), f32),
             pltpu.VMEM((3, batches, rows, width), bf16),
             pltpu.VMEM((3, batches, rows, width), bf16),
+            pltpu.VMEM((2, 2 * rows, width), bf16),
+            pltpu.VMEM((2, 2 * rows, width), bf16),
+            pltpu.VMEM((2, 2 * rows, width), f32),
             pltpu.SemaphoreType.DMA((4,)),
             pltpu.SemaphoreType.DMA((width // TILE,)),
             pltpu.SemaphoreType.DMA((ranks,)),
@@ -343,6 +375,8 @@
             pltpu.SemaphoreType.DMA((parts, batches)),
             pltpu.SemaphoreType.DMA((3, batches)),
             pltpu.SemaphoreType.DMA((3, batches)),
+            pltpu.SemaphoreType.DMA((2,)),
+            pltpu.SemaphoreType.DMA((2,)),
         ],
         compiler_params=pltpu.CompilerParams(
             collective_id=0, has_side_effects=True, vmem_limit_bytes=48 * 1024 * 1024

time: 30.7 us -> 27.5 us (0.90)
  Pallas kernels: 29.9 us -> 26.6 us
    pallas_call x1, Pallas kernels: 29.9 us -> 26.6 us  [dense_shards(): pl.pallas_call(functools.partial(dense_kernel, sizes), out_shape=jax.Shap...]
where the time goes in v6:
time: 27.5 us; the launch traced here: 27.3 us
  Pallas kernels  26.6 us (97%)
  local copies, waits for them, and re-layouts  0.66 us (2%)
    pallas_call x1, Pallas kernels, dense_shards(): pl.pallas_call(functools.partial(dense_kernel, sizes), out_shape=jax.Shap...  26.6 us
    unnamed x1, local copies, waits for them, and re-layouts  0.66 us

profile of v6, /device:TPU:0, one launch (start us, length us, event | category | flops | bytes accessed | tf_op | source)
XLA Modules:
  0.0 27.3 jit_solution(11900704991383910192)
XLA Ops:
  0.0 26.6 %shard_map.55 = bf16[2,16,2048]{2,1,0:T(8,128)(2,1)S(1)} custom-call(bf16[2,256,768]{2,1,0:T(8,128)(2,1)} %bitcast.5, bf16[768,2048]{1,0:T(8,128)(2,1)} %bitcast.4, s32[2,8,16]{2,1,0:T(8,128)} %bitcast.6, f32[2,8,16]{2,1,0:T(8,128)} %bitcast.7, bf16[2,16,2048]{2,1,0:T(8,128)(2,1)} %residual_hbm.1), custom_call_target="tpu_custom_call" | custom-call | tf_op jit(solution)/shard_map/pallas_call | solution.py:342
  26.6 0.7 %copy.7 = bf16[2,16,2048]{2,1,0:T(8,128)(2,1)} copy(bf16[2,16,2048]{2,1,0:T(8,128)(2,1)S(1)} %shard_map.55) | data formatting | bytes 262144

commit v7 on v6

--- a/solution.py
+++ b/solution.py
@@ -72,8 +72,9 @@
     hidden, weight, routes, shares, residual, produced,
     note_out, note_in, slot_of,
     core_out, core_in, core_kept, x_out, x_in, x_kept, z_out, z_in, near_out, near_in, near_kept,
+    side_out, side_in, side_kept, far_out, far_in,
     load_sem, column_sem, note_send, note_recv, core_send, core_recv, x_send, x_recv, z_send, z_recv,
-    near_send, near_recv,
+    near_send, near_recv, side_send, side_recv, far_send, far_recv,
 ):
     ranks, batches, rows, chosen, slots, width = sizes
     both = batches * rows
@@ -87,13 +88,21 @@
 
     barrier = pltpu.get_barrier_semaphore()
 
+    turn = 2 * (me // (ranks // 2)) - 1
+
+    def peer_of(step):
+        return lax.rem(2 * ranks - 1 - me + turn * step, ranks)
+
     def greet(step, carry):
-        pl.semaphore_signal(
-            barrier, inc=1, device_id={"ep": lax.rem(me + step, ranks)}, device_id_type=MESH
-        )
+        peer = peer_of(step)
+
+        @pl.when(peer != me)
+        def _():
+            pl.semaphore_signal(barrier, inc=1, device_id={"ep": peer}, device_id_type=MESH)
+
         return carry
 
-    lax.fori_loop(1, ranks, greet, 0)
+    lax.fori_loop(0, ranks, greet, 0)
 
     loads = [
         pltpu.make_async_copy(routes_hbm, routes, load_sem.at[0]),
@@ -126,8 +135,7 @@
 
     pl.semaphore_wait(barrier, ranks - 1)
 
-    def note_to(step):
-        peer = lax.rem(me + step, ranks)
+    def note_to(peer):
         return pltpu.make_async_remote_copy(
             src_ref=note_out.at[peer],
             dst_ref=note_in.at[me],
@@ -149,10 +157,15 @@
         )
 
     def send_note(step, carry):
-        note_to(step).start()
+        peer = peer_of(step)
+
+        @pl.when(peer != me)
+        def _():
+            note_to(peer).start()
+
         return carry
 
-    lax.fori_loop(1, ranks, send_note, 0)
+    lax.fori_loop(0, ranks, send_note, 0)
 
     def produce(b, tiles):
         for j in tiles:
@@ -163,6 +176,7 @@
             ).astype(jnp.bfloat16)
 
     tiles = width // TILE
+    spans = (width, width // 2)
     loads[2].wait()
     produce(0, range(tiles))
     produce(1, range(tiles))
@@ -203,15 +217,17 @@
         )
 
     def x_copy(i, b):
-        return pltpu.make_async_remote_copy(
-            src_ref=x_out.at[i, b], dst_ref=x_in.at[i, b],
+        cut = pl.ds(0, spans[b])
+        return pltpu.make_async_remote_copy(
+            src_ref=x_out.at[i, b, :, cut], dst_ref=x_in.at[i, b, :, cut],
             send_sem=x_send.at[i, b], recv_sem=x_recv.at[i, b],
             device_id={"ep": beside}, device_id_type=MESH,
         )
 
     def z_copy(i, b):
-        return pltpu.make_async_remote_copy(
-            src_ref=z_out.at[i, b], dst_ref=z_in.at[i, b],
+        cut = pl.ds(0, spans[b])
+        return pltpu.make_async_remote_copy(
+            src_ref=z_out.at[i, b, :, cut], dst_ref=z_in.at[i, b, :, cut],
             send_sem=z_send.at[i, b], recv_sem=z_recv.at[i, b],
             device_id={"ep": far if i == 1 else near}, device_id_type=MESH,
         )
@@ -254,42 +270,72 @@
             device_id={"ep": near}, device_id_type=MESH,
         )
 
+    def side_copy(k):
+        return pltpu.make_async_remote_copy(
+            src_ref=side_out.at[k], dst_ref=side_in.at[k],
+            send_sem=side_send.at[k], recv_sem=side_recv.at[k],
+            device_id={"ep": beside}, device_id_type=MESH,
+        )
+
+    def far_copy():
+        return pltpu.make_async_remote_copy(
+            src_ref=far_out.at[0], dst_ref=far_in.at[0],
+            send_sem=far_send.at[0], recv_sem=far_recv.at[0],
+            device_id={"ep": far}, device_id_type=MESH,
+        )
+
     def over_cores(i, b):
         core_copy(i, b).wait_recv()
-        total = core_kept[i, b] + core_in[i, b].astype(jnp.float32)
-        if b == 0:
-            x_out[i, b] = total[:rows].astype(jnp.bfloat16)
-            x_kept[i, b] = total[rows:]
-            x_copy(i, b).start()
-        elif i % 2 == 0:
-            near_out[i // 2] = total.astype(jnp.bfloat16)
-            near_copy(i // 2).start()
+        n = spans[b]
+        total = core_kept[i, b, :, :n] + core_in[i, b, :, :n].astype(jnp.float32)
+        x_out[i, b, :, :n] = total[:rows].astype(jnp.bfloat16)
+        x_kept[i, b, :, :n] = total[rows:]
+        x_copy(i, b).start()
+        if b == 1:
+            total = core_kept[i, b, :, n:] + core_in[i, b, :, n:].astype(jnp.float32)
+            if i % 2 == 0:
+                near_out[i // 2] = total.astype(jnp.bfloat16)
+                near_copy(i // 2).start()
+            else:
+                near_kept[i // 2] = total
+
+    def over_near(k):
+        near_copy(k).wait_recv()
+        total = near_kept[k] + near_in[k].astype(jnp.float32)
+        side_out[k] = total[:rows].astype(jnp.bfloat16)
+        side_kept[k] = total[rows:]
+        side_copy(k).start()
+
+    def over_side(k):
+        side_copy(k).wait_recv()
+        total = side_kept[k] + side_in[k].astype(jnp.float32)
+        if k == 0:
+            far_out[0] = total.astype(jnp.bfloat16)
+            far_copy().start()
         else:
-            near_kept[i // 2] = total
-
-    def over_near(i):
-        near_copy(i // 2).wait_recv()
-        total = near_kept[i // 2] + near_in[i // 2].astype(jnp.float32)
-        x_out[i, 1] = total[:rows].astype(jnp.bfloat16)
-        x_kept[i, 1] = total[rows:]
-        x_copy(i, 1).start()
+            n = spans[1]
+            total = total + residual[1, :, n:].astype(jnp.float32)
+            far_copy().wait_recv()
+            mixed_ref[1, :, n:] = (total + far_in[0].astype(jnp.float32)).astype(jnp.bfloat16)
 
     def over_x(i, b):
+        n = spans[b]
         x_copy(i, b).wait_recv()
-        total = x_kept[i, b] + x_in[i, b].astype(jnp.float32)
-        if i == 1 and b == 0:
+        total = x_kept[i, b, :, :n] + x_in[i, b, :, :n].astype(jnp.float32)
+        if i == 1:
             z_copy(0, b).wait_recv()
-            total = total + z_in[0, b].astype(jnp.float32)
+            total = total + z_in[0, b, :, :n].astype(jnp.float32)
         if i < 3:
-            z_out[i, b] = total.astype(jnp.bfloat16)
+            z_out[i, b, :, :n] = total.astype(jnp.bfloat16)
             z_copy(i, b).start()
         else:
-            total = total + residual[b].astype(jnp.float32)
-            if b == 0:
-                z_copy(2, b).wait_recv()
-                total = total + z_in[2, b].astype(jnp.float32)
+            total = total + residual[b, :, :n].astype(jnp.float32)
+            z_copy(2, b).wait_recv()
+            total = total + z_in[2, b, :, :n].astype(jnp.float32)
             z_copy(1, b).wait_recv()
-            mixed_ref[b] = (total + z_in[1, b].astype(jnp.float32)).astype(jnp.bfloat16)
+            mixed_ref[b, :, :n] = (total + z_in[1, b, :, :n].astype(jnp.float32)).astype(
+                jnp.bfloat16
+            )
 
     spread((0, 1), 0)
     spread((0, 1), 1)
@@ -302,30 +348,34 @@
     over_x(0, 0)
     over_cores(3, 0)
     spread((2, 3), 1)
-    over_near(1)
+    over_near(0)
     over_cores(2, 1)
     over_cores(3, 1)
+    over_x(0, 1)
     over_x(1, 0)
+    over_x(1, 1)
+    over_near(1)
     over_x(2, 0)
-    over_x(1, 1)
-    over_near(3)
+    over_side(0)
+    over_x(2, 1)
     residual_load.wait()
     over_x(3, 0)
     over_x(3, 1)
-
-    for i in range(4):
-        for b in range(batches):
+    over_side(1)
+
+    for b in range(batches):
+        for i in range(4):
             core_copy(i, b).wait_send()
-        x_copy(i, 0).wait_send()
+            x_copy(i, b).wait_send()
+            if i < 3:
+                z_copy(i, b).wait_send()
     for k in range(2):
         near_copy(k).wait_send()
-        x_copy(2 * k + 1, 1).wait_send()
-    for i in range(3):
-        z_copy(i, 0).wait_send()
-    z_copy(1, 1).wait_send()
+        side_copy(k).wait_send()
+    far_copy().wait_send()
 
     def note_left(step, carry):
-        note_to(step).wait_send()
+        note_to(lax.rem(me + step, ranks)).wait_send()
         return carry
 
     lax.fori_loop(1, ranks, note_left, 0)
@@ -362,9 +412,14 @@
             pltpu.VMEM((parts, batches, rows, width), f32),
             pltpu.VMEM((3, batches, rows, width), bf16),
             pltpu.VMEM((3, batches, rows, width), bf16),
-            pltpu.VMEM((2, 2 * rows, width), bf16),
-            pltpu.VMEM((2, 2 * rows, width), bf16),
-            pltpu.VMEM((2, 2 * rows, width), f32),
+            pltpu.VMEM((2, 2 * rows, width // 2), bf16),
+            pltpu.VMEM((2, 2 * rows, width // 2), bf16),
+            pltpu.VMEM((2, 2 * rows, width // 2), f32),
+            pltpu.VMEM((2, rows, width // 2), bf16),
+            pltpu.VMEM((2, rows, width // 2), bf16),
+            pltpu.VMEM((2, rows, width // 2), f32),
+            pltpu.VMEM((1, rows, width // 2), bf16),
+            pltpu.VMEM((1, rows, width // 2), bf16),
             pltpu.SemaphoreType.DMA((4,)),
             pltpu.SemaphoreType.DMA((width // TILE,)),
             pltpu.SemaphoreType.DMA((ranks,)),
@@ -377,6 +432,10 @@
             pltpu.SemaphoreType.DMA((3, batches)),
             pltpu.SemaphoreType.DMA((2,)),
             pltpu.SemaphoreType.DMA((2,)),
+            pltpu.SemaphoreType.DMA((2,)),
+            pltpu.SemaphoreType.DMA((2,)),
+            pltpu.SemaphoreType.DMA((1,)),
+            pltpu.SemaphoreType.DMA((1,)),
         ],
         compiler_params=pltpu.CompilerParams(
             collective_id=0, has_side_effects=True, vmem_limit_bytes=48 * 1024 * 1024

time: 27.5 us -> 28.2 us (1.025)
  Pallas kernels: 26.6 us -> 27.3 us
    pallas_call x1, Pallas kernels: 26.6 us -> 27.3 us  [dense_shards(): pl.pallas_call(functools.partial(dense_kernel, sizes), out_shape=jax.Shap...]
where the time goes in v7:
time: 28.2 us; the launch traced here: 28 us
  Pallas kernels  27.3 us (97%)
  local copies, waits for them, and re-layouts  0.66 us (2%)
    pallas_call x1, Pallas kernels, dense_shards(): pl.pallas_call(functools.partial(dense_kernel, sizes), out_shape=jax.Shap...  27.3 us
    unnamed x1, local copies, waits for them, and re-layouts  0.66 us

profile of v7, /device:TPU:0, one launch (start us, length us, event | category | flops | bytes accessed | tf_op | source)
XLA Modules:
  0.0 28.0 jit_solution(17156151839278260640)
XLA Ops:
  0.0 27.3 %shard_map.55 = bf16[2,16,2048]{2,1,0:T(8,128)(2,1)S(1)} custom-call(bf16[2,256,768]{2,1,0:T(8,128)(2,1)} %bitcast.5, bf16[768,2048]{1,0:T(8,128)(2,1)} %bitcast.4, s32[2,8,16]{2,1,0:T(8,128)} %bitcast.6, f32[2,8,16]{2,1,0:T(8,128)} %bitcast.7, bf16[2,16,2048]{2,1,0:T(8,128)(2,1)} %residual_hbm.1), custom_call_target="tpu_custom_call" | custom-call | tf_op jit(solution)/shard_map/pallas_call | solution.py:392
  27.4 0.7 %copy.7 = bf16[2,16,2048]{2,1,0:T(8,128)(2,1)} copy(bf16[2,16,2048]{2,1,0:T(8,128)(2,1)S(1)} %shard_map.55) | data formatting | bytes 262144

commit v8 on v6

--- a/solution.py
+++ b/solution.py
@@ -87,13 +87,21 @@
 
     barrier = pltpu.get_barrier_semaphore()
 
+    turn = 2 * (me // (ranks // 2)) - 1
+
+    def peer_of(step):
+        return lax.rem(2 * ranks - 1 - me + turn * step, ranks)
+
     def greet(step, carry):
-        pl.semaphore_signal(
-            barrier, inc=1, device_id={"ep": lax.rem(me + step, ranks)}, device_id_type=MESH
-        )
+        peer = peer_of(step)
+
+        @pl.when(peer != me)
+        def _():
+            pl.semaphore_signal(barrier, inc=1, device_id={"ep": peer}, device_id_type=MESH)
+
         return carry
 
-    lax.fori_loop(1, ranks, greet, 0)
+    lax.fori_loop(0, ranks, greet, 0)
 
     loads = [
         pltpu.make_async_copy(routes_hbm, routes, load_sem.at[0]),
@@ -126,8 +134,7 @@
 
     pl.semaphore_wait(barrier, ranks - 1)
 
-    def note_to(step):
-        peer = lax.rem(me + step, ranks)
+    def note_to(peer):
         return pltpu.make_async_remote_copy(
             src_ref=note_out.at[peer],
             dst_ref=note_in.at[me],
@@ -149,10 +156,15 @@
         )
 
     def send_note(step, carry):
-        note_to(step).start()
+        peer = peer_of(step)
+
+        @pl.when(peer != me)
+        def _():
+            note_to(peer).start()
+
         return carry
 
-    lax.fori_loop(1, ranks, send_note, 0)
+    lax.fori_loop(0, ranks, send_note, 0)
 
     def produce(b, tiles):
         for j in tiles:
@@ -305,30 +317,31 @@
     over_near(1)
     over_cores(2, 1)
     over_cores(3, 1)
+    def note_left(step, carry):
+        note_to(lax.rem(me + step, ranks)).wait_send()
+        return carry
+
     over_x(1, 0)
+    lax.fori_loop(1, ranks, note_left, 0)
     over_x(2, 0)
+    for i in range(4):
+        for b in range(batches):
+            core_copy(i, b).wait_send()
     over_x(1, 1)
     over_near(3)
     residual_load.wait()
-    over_x(3, 0)
-    over_x(3, 1)
-
     for i in range(4):
-        for b in range(batches):
-            core_copy(i, b).wait_send()
         x_copy(i, 0).wait_send()
     for k in range(2):
         near_copy(k).wait_send()
-        x_copy(2 * k + 1, 1).wait_send()
-    for i in range(3):
-        z_copy(i, 0).wait_send()
+    over_x(3, 0)
+    z_copy(0, 0).wait_send()
+    z_copy(2, 0).wait_send()
+    x_copy(1, 1).wait_send()
+    over_x(3, 1)
+    x_copy(3, 1).wait_send()
+    z_copy(1, 0).wait_send()
     z_copy(1, 1).wait_send()
-
-    def note_left(step, carry):
-        note_to(step).wait_send()
-        return carry
-
-    lax.fori_loop(1, ranks, note_left, 0)
 
 
 def dense_shards(ranks, hidden, down_weight, routes, route_weight, residual):

time: 27.5 us -> 27.4 us (level)
  no operation moved by 1% of the time
where the time goes in v8:
time: 27.4 us; the launch traced here: 27.2 us
  Pallas kernels  26.5 us (97%)
  local copies, waits for them, and re-layouts  0.66 us (2%)
    pallas_call x1, Pallas kernels, dense_shards(): pl.pallas_call(functools.partial(dense_kernel, sizes), out_shape=jax.Shap...  26.5 us
    unnamed x1, local copies, waits for them, and re-layouts  0.66 us

profile of v8, /device:TPU:0, one launch (start us, length us, event | category | flops | bytes accessed | tf_op | source)
XLA Modules:
  0.0 27.2 jit_solution(16090368033035264347)
XLA Ops:
  0.0 26.5 %shard_map.55 = bf16[2,16,2048]{2,1,0:T(8,128)(2,1)S(1)} custom-call(bf16[2,256,768]{2,1,0:T(8,128)(2,1)} %bitcast.5, bf16[768,2048]{1,0:T(8,128)(2,1)} %bitcast.4, s32[2,8,16]{2,1,0:T(8,128)} %bitcast.6, f32[2,8,16]{2,1,0:T(8,128)} %bitcast.7, bf16[2,16,2048]{2,1,0:T(8,128)(2,1)} %residual_hbm.1), custom_call_target="tpu_custom_call" | custom-call | tf_op jit(solution)/shard_map/pallas_call | solution.py:355
  26.5 0.7 %copy.7 = bf16[2,16,2048]{2,1,0:T(8,128)(2,1)} copy(bf16[2,16,2048]{2,1,0:T(8,128)(2,1)S(1)} %shard_map.55) | data formatting | bytes 262144

commit v9 on v8

--- a/solution.py
+++ b/solution.py
@@ -101,8 +101,6 @@
 
         return carry
 
-    lax.fori_loop(0, ranks, greet, 0)
-
     loads = [
         pltpu.make_async_copy(routes_hbm, routes, load_sem.at[0]),
         pltpu.make_async_copy(shares_hbm, shares, load_sem.at[1]),
@@ -115,7 +113,10 @@
         for j in range(width // TILE)
     ]
     residual_load = pltpu.make_async_copy(residual_hbm, residual, load_sem.at[3])
-    for copy in loads + columns + [residual_load]:
+    loads[0].start()
+    loads[1].start()
+    lax.fori_loop(0, ranks, greet, 0)
+    for copy in loads[2:] + columns + [residual_load]:
         copy.start()
 
     loads[0].wait()
@@ -303,20 +304,21 @@
             z_copy(1, b).wait_recv()
             mixed_ref[b] = (total + z_in[1, b].astype(jnp.float32)).astype(jnp.bfloat16)
 
+    spread((0, 1), 1)
     spread((0, 1), 0)
-    spread((0, 1), 1)
+    over_cores(0, 1)
     over_cores(0, 0)
-    over_cores(0, 1)
     over_cores(1, 0)
+    spread((2, 3), 1)
     over_cores(1, 1)
     spread((2, 3), 0)
+    over_cores(2, 1)
+    over_x(0, 0)
     over_cores(2, 0)
-    over_x(0, 0)
     over_cores(3, 0)
-    spread((2, 3), 1)
+    over_cores(3, 1)
     over_near(1)
-    over_cores(2, 1)
-    over_cores(3, 1)
+
     def note_left(step, carry):
         note_to(lax.rem(me + step, ranks)).wait_send()
         return carry

time: 27.4 us -> 30.3 us (1.11)
  Pallas kernels: 26.5 us -> 29.4 us
    pallas_call x1, Pallas kernels: 26.5 us -> 29.4 us  [dense_shards(): pl.pallas_call(functools.partial(dense_kernel, sizes), out_shape=jax.Shap...]
where the time goes in v9:
time: 30.3 us; the launch traced here: 30.1 us
  Pallas kernels  29.4 us (97%)
  local copies, waits for them, and re-layouts  0.66 us (2%)
    pallas_call x1, Pallas kernels, dense_shards(): pl.pallas_call(functools.partial(dense_kernel, sizes), out_shape=jax.Shap...  29.4 us
    unnamed x1, local copies, waits for them, and re-layouts  0.66 us

profile of v9, /device:TPU:0, one launch (start us, length us, event | category | flops | bytes accessed | tf_op | source)
XLA Modules:
  0.0 30.1 jit_solution(15463122585874394795)
XLA Ops:
  0.0 29.4 %shard_map.55 = bf16[2,16,2048]{2,1,0:T(8,128)(2,1)S(1)} custom-call(bf16[2,256,768]{2,1,0:T(8,128)(2,1)} %bitcast.5, bf16[768,2048]{1,0:T(8,128)(2,1)} %bitcast.4, s32[2,8,16]{2,1,0:T(8,128)} %bitcast.6, f32[2,8,16]{2,1,0:T(8,128)} %bitcast.7, bf16[2,16,2048]{2,1,0:T(8,128)(2,1)} %residual_hbm.1), custom_call_target="tpu_custom_call" | custom-call | tf_op jit(solution)/shard_map/pallas_call | solution.py:357
  29.4 0.7 %copy.7 = bf16[2,16,2048]{2,1,0:T(8,128)(2,1)} copy(bf16[2,16,2048]{2,1,0:T(8,128)(2,1)S(1)} %shard_map.55) | data formatting | bytes 262144

commit v10 on v8

--- a/solution.py
+++ b/solution.py
@@ -101,8 +101,6 @@
 
         return carry
 
-    lax.fori_loop(0, ranks, greet, 0)
-
     loads = [
         pltpu.make_async_copy(routes_hbm, routes, load_sem.at[0]),
         pltpu.make_async_copy(shares_hbm, shares, load_sem.at[1]),
@@ -115,7 +113,10 @@
         for j in range(width // TILE)
     ]
     residual_load = pltpu.make_async_copy(residual_hbm, residual, load_sem.at[3])
-    for copy in loads + columns + [residual_load]:
+    loads[0].start()
+    loads[1].start()
+    lax.fori_loop(0, ranks, greet, 0)
+    for copy in loads[2:] + columns + [residual_load]:
         copy.start()
 
     loads[0].wait()
@@ -306,8 +307,8 @@
     spread((0, 1), 0)
     spread((0, 1), 1)
     over_cores(0, 0)
+    over_cores(1, 0)
     over_cores(0, 1)
-    over_cores(1, 0)
     over_cores(1, 1)
     spread((2, 3), 0)
     over_cores(2, 0)

time: 27.4 us -> 27.4 us (level)
  no operation moved by 1% of the time
where the time goes in v10:
time: 27.4 us; the launch traced here: 27.2 us
  Pallas kernels  26.5 us (97%)
  local copies, waits for them, and re-layouts  0.66 us (2%)
    pallas_call x1, Pallas kernels, dense_shards(): pl.pallas_call(functools.partial(dense_kernel, sizes), out_shape=jax.Shap...  26.5 us
    unnamed x1, local copies, waits for them, and re-layouts  0.66 us

profile of v10, /device:TPU:0, one launch (start us, length us, event | category | flops | bytes accessed | tf_op | source)
XLA Modules:
  0.0 27.2 jit_solution(7502125253232773229)
XLA Ops:
  0.0 26.5 %shard_map.55 = bf16[2,16,2048]{2,1,0:T(8,128)(2,1)S(1)} custom-call(bf16[2,256,768]{2,1,0:T(8,128)(2,1)} %bitcast.5, bf16[768,2048]{1,0:T(8,128)(2,1)} %bitcast.4, s32[2,8,16]{2,1,0:T(8,128)} %bitcast.6, f32[2,8,16]{2,1,0:T(8,128)} %bitcast.7, bf16[2,16,2048]{2,1,0:T(8,128)(2,1)} %residual_hbm.1), custom_call_target="tpu_custom_call" | custom-call | tf_op jit(solution)/shard_map/pallas_call | solution.py:356
  26.6 0.7 %copy.7 = bf16[2,16,2048]{2,1,0:T(8,128)(2,1)} copy(bf16[2,16,2048]{2,1,0:T(8,128)(2,1)S(1)} %shard_map.55) | data formatting | bytes 262144
